TPU v7x, 256 devices: a whole 4x4x8 slice. The times are simulated.
256 devices in a mesh: grp: 4 (over z_hi, core), pos: 64 (over z_lo, x, y).
Axes of the slice: x: 4, y: 4, z: 8 (z_hi: 2, z_lo: 4; z = z_hi * 4 + z_lo), core: 2. Of those that a mesh axis runs over, the one named last changes fastest.
Arguments:
- query: float32 [256, 131072], P(None, ('grp', 'pos')), may hold values from -6 to 6
- key_branch: float32 [256, 131072], P(None, ('grp', 'pos')), may hold values from -6 to 6
- value_branch: float32 [256, 131072], P(None, ('grp', 'pos')), may hold values from -6 to 6
- long_filter: float32 [256, 131072], P(None, ('grp', 'pos')), may hold values from -0.015625 to 0.015625
- skip_gain: float32 [256], replicated, may hold values from -4 to 4
Outputs:
- mixed: float32 [256, 131072], P(None, ('grp', 'pos'))
All inputs are finite; a program needn't handle non-finite values.
Results may differ from a plain program's by a relative error of at most 0.000062.
Values sent between devices are 32-bit elements; how exact they have to be, the bound alone decides.
No kernel may reach another device: no remote copies, remote signals or barrier semaphores. Data moves between devices by JAX's collectives and lax.ppermute only.
A program may use at most 64 MiB of HBM per device.

v0:
```python
import math

import jax
import jax.numpy as jnp
from jax import lax
from jax.sharding import PartitionSpec as P

precise = lax.Precision.HIGHEST


def from_partner(block, axis, stride):
    count = lax.axis_size(axis)
    route = []
    for low in range(count):
        high = low | 1 << stride
        if high != low and high < count:
            route += [(low, high), (high, low)]
    return lax.ppermute(block, axis, route)


def unit_turns(exponent, period, direction):
    angle = direction * 2.0 * math.pi / period * exponent.astype(jnp.float32)
    return (jnp.cos(angle), jnp.sin(angle))


def rotate_by(values, cos_part, sin_part):
    return jnp.stack(
        [values[0] * cos_part - values[1] * sin_part, values[0] * sin_part + values[1] * cos_part]
    )


def dft_apply(pattern, cos_part, sin_part, values):
    real_part = jnp.einsum(pattern, cos_part, values[0], precision=precise) - jnp.einsum(
        pattern, sin_part, values[1], precision=precise
    )
    imag_part = jnp.einsum(pattern, sin_part, values[0], precision=precise) + jnp.einsum(
        pattern, cos_part, values[1], precision=precise
    )
    return jnp.stack([real_part, imag_part])


def dft_table(count_size, direction):
    steps_along = jnp.arange(count_size, dtype=jnp.int32)
    return unit_turns(
        steps_along[:, None] * steps_along[None, :] % count_size, count_size, direction
    )


def halves(signal, positions, length):
    cos_part, sin_part = unit_turns(positions, 2 * length, -1.0)
    real_part = jnp.stack([signal, signal * cos_part])
    imag_part = jnp.stack([jnp.zeros_like(signal), signal * sin_part])
    return jnp.stack([real_part, imag_part])


def fold_real(values, positions, length):
    cos_part, sin_part = unit_turns(positions, 2 * length, 1.0)
    return (values[0, 0] + values[0, 1] * cos_part - values[1, 1] * sin_part)[None]


def body(query, key_branch, value_branch, long_filter, skip_gain):
    channel_count, line_width = query.shape
    group_count = lax.axis_size("grp")
    line_count = lax.axis_size("pos")
    group_index = lax.axis_index("grp")
    line_index = lax.axis_index("pos")
    devices = group_count * line_count
    length = devices * line_width
    bit_count = group_count.bit_length() - 1
    top_bit = bit_count - 1
    line_piece = line_width // line_count
    first_radix = 64
    second_radix = line_width // first_radix
    gated_input = key_branch * value_branch
    signal = jnp.concatenate([gated_input, long_filter], 0)
    offsets = jnp.arange(line_width, dtype=jnp.int32)
    own_start = line_width * (group_index * line_count + line_index)
    partner_start = line_width * ((group_index ^ 1 << top_bit) * line_count + line_index)
    partner_signal = from_partner(signal, "grp", top_bit)
    own_halves = halves(signal, own_start + offsets, length)
    other_halves = halves(partner_signal, partner_start + offsets, length)
    upper_bit = group_index >> top_bit & 1
    spectra = jnp.where(upper_bit == 0, own_halves + other_halves, other_halves - own_halves)
    cos_part, sin_part = unit_turns(upper_bit * (group_index % (1 << top_bit)), 2 << top_bit, -1.0)
    spectra = rotate_by(spectra, cos_part, sin_part)
    section_bit = 0
    partner = from_partner(spectra, "grp", section_bit)
    upper_bit = group_index >> section_bit & 1
    spectra = jnp.where(upper_bit == 0, spectra + partner, partner - spectra)
    cos_part, sin_part = unit_turns(
        upper_bit * (group_index % (1 << section_bit)), 2 << section_bit, -1.0
    )
    spectra = rotate_by(spectra, cos_part, sin_part)
    first_freq = jnp.int32(0)
    for section_bit in range(bit_count):
        first_freq = first_freq + ((group_index >> section_bit & 1) << bit_count - 1 - section_bit)
    cos_part, sin_part = unit_turns(line_index * first_freq, devices, -1.0)
    spectra = rotate_by(spectra, cos_part, sin_part)
    block_values = lax.all_to_all(spectra, "pos", split_axis=3, concat_axis=3, tiled=True)
    row_count = block_values.shape[2]
    shaped = block_values.reshape(2, 2, row_count, line_count, line_piece)
    cos_line, sin_line = dft_table(line_count, -1.0)
    mixed_line = dft_apply("kp,hrpq->hrkq", cos_line, sin_line, shaped)
    spectra = lax.all_to_all(
        mixed_line.reshape(2, 2, row_count, line_width),
        "pos",
        split_axis=3,
        concat_axis=3,
        tiled=True,
    )
    freq_index = group_count * line_index + first_freq
    cos_part, sin_part = unit_turns(offsets * freq_index, length, -1.0)
    spectra = rotate_by(spectra, cos_part, sin_part)
    radix_grid = (
        jnp.arange(first_radix, dtype=jnp.int32)[:, None]
        * jnp.arange(second_radix, dtype=jnp.int32)[None, :]
    )
    row_total = spectra.shape[2]
    shaped = spectra.reshape(2, 2, row_total, first_radix, second_radix)
    cos_first, sin_first = dft_table(first_radix, -1.0)
    section_one = dft_apply("ma,hrab->hrmb", cos_first, sin_first, shaped)
    cos_grid, sin_grid = unit_turns(radix_grid, line_width, -1.0)
    section_one = rotate_by(section_one, cos_grid, sin_grid)
    cos_second, sin_second = dft_table(second_radix, -1.0)
    spectra = dft_apply("nb,hrmb->hrmn", cos_second, sin_second, section_one)
    source_part = spectra[:, :, :channel_count]
    filter_part = spectra[:, :, channel_count:]
    product = rotate_by(source_part, filter_part[0], filter_part[1])
    inverse_rows = product.shape[2]
    cos_second, sin_second = dft_table(second_radix, 1.0)
    section_one = dft_apply("bn,hcmn->hcmb", cos_second, sin_second, product)
    cos_grid, sin_grid = unit_turns(radix_grid, line_width, 1.0)
    section_one = rotate_by(section_one, cos_grid, sin_grid)
    cos_first, sin_first = dft_table(first_radix, 1.0)
    product = dft_apply("am,hcmb->hcab", cos_first, sin_first, section_one)
    product = product.reshape(2, 2, inverse_rows, line_width)
    cos_part, sin_part = unit_turns(offsets * freq_index, length, 1.0)
    product = rotate_by(product, cos_part, sin_part)
    block_values = lax.all_to_all(product, "pos", split_axis=3, concat_axis=3, tiled=True)
    row_count = block_values.shape[2]
    shaped_line = block_values.reshape(2, 2, row_count, line_count, line_piece)
    cos_line, sin_line = dft_table(line_count, 1.0)
    mixed_line = dft_apply("pk,hrkq->hrpq", cos_line, sin_line, shaped_line)
    product = lax.all_to_all(
        mixed_line.reshape(2, 2, row_count, line_width),
        "pos",
        split_axis=3,
        concat_axis=3,
        tiled=True,
    )
    cos_part, sin_part = unit_turns(line_index * first_freq, devices, 1.0)
    product = rotate_by(product, cos_part, sin_part)
    section_bit = 0
    upper_bit = group_index >> section_bit & 1
    cos_part, sin_part = unit_turns(
        upper_bit * (group_index % (1 << section_bit)), 2 << section_bit, 1.0
    )
    product = rotate_by(product, cos_part, sin_part)
    partner = from_partner(product, "grp", section_bit)
    product = jnp.where(upper_bit == 0, product + partner, partner - product)
    upper_bit = group_index >> top_bit & 1
    cos_part, sin_part = unit_turns(upper_bit * (group_index % (1 << top_bit)), 2 << top_bit, 1.0)
    product = rotate_by(product, cos_part, sin_part)
    own_fold = fold_real(product, own_start + offsets, length)
    sent_fold = fold_real(product, partner_start + offsets, length)
    partner_fold = from_partner(sent_fold, "grp", top_bit)
    convolved = jnp.where(upper_bit == 0, own_fold + partner_fold, partner_fold - own_fold)
    convolved = convolved.reshape(channel_count, line_width) / (2.0 * length)
    return query * (convolved + skip_gain[:, None] * gated_input)


def solution(mesh):
    return jax.shard_map(
        body,
        mesh=mesh,
        in_specs=(
            P(None, ("grp", "pos")),
            P(None, ("grp", "pos")),
            P(None, ("grp", "pos")),
            P(None, ("grp", "pos")),
            P(),
        ),
        out_specs=P(None, ("grp", "pos")),
        check_vma=False,
    )
```

profile of v0, /device:TPU:16, one launch (start us, length us, event | category | flops | bytes accessed | tf_op | source)
XLA Modules:
  0.0 530.8 jit_solution(12897774600141976741)
XLA Ops:
  1.3 2.3 fusion.263
  3.6 7.2 %collective-permute-start = (f32[512,512]{1,0:T(8,128)}, f32[512,512]{1,0:T(8,128)S(1)}, u32[]{:S(2)}, u32[]{:S(2)}) collective-permute-start(f32[512,512]{1,0:T(8,128)} %get-tuple-element.33), channel_id=1, source_target_pairs={{0,128},{128,0},{64,192},{192,64},{1,129},{129,1},{65,193},{193,65... | collective-permute-start | bytes 3145736 | tf_op jit(solution)/shard_map/ppermute | solution.py:18
  11.8 43.7 %collective-permute-done = f32[512,512]{1,0:T(8,128)S(1)} collective-permute-done((f32[512,512]{1,0:T(8,128)}, f32[512,512]{1,0:T(8,128)S(1)}, u32[]{:S(2)}, u32[]{:S(2)}) %collective-permute-start) | collective-permute-done | bytes 1048608 | tf_op jit(solution)/shard_map/ppermute | solution.py:18
  57.9 2.6 pad_maximum_fusion.2
  60.7 7.3 %collective-permute-done.1 = f32[2,2,512,512]{3,2,1,0:T(8,128)} collective-permute-done((f32[2,2,512,512]{3,2,1,0:T(8,128)}, f32[2,2,512,512]{3,2,1,0:T(8,128)}, u32[]{:S(2)}, u32[]{:S(2)}) %collective-permute-start.1) | collective-permute-done | bytes 4194336 | tf_op jit(solution)/shard_map/ppermute | solution.py:18
  68.1 3.9 subtract_select_fusion
  72.7 2.4 pad_maximum_fusion.3
  75.1 7.3 %copy.98 = f32[2,2,512,512]{2,1,0,3:T(2,128)} copy(f32[2,2,512,512]{3,2,1,0:T(8,128)} %pad_maximum_fusion.3) | data formatting | bytes 8388608 | tf_op jit(solution)/shard_map/stack | solution.py:27
  82.4 105.6 %all_to_all.20 = f32[2,2,512,512]{2,1,0,3:T(2,128)S(1)} all-to-all(f32[2,2,512,512]{2,1,0,3:T(2,128)} %copy.98), channel_id=1, replica_groups=mesh['grp'=4,'pos'=64] {'pos'}, dimensions={3} | all-to-all | bytes 8388608 | tf_op jit(solution)/shard_map/all_to_all | solution.py:99
  188.0 1.4 fusion.265
  189.8 3.4 fusion.20
  193.2 3.4 fusion.18
  197.1 3.8 subtract_bitcast_fusion.1
  202.1 3.6 add_bitcast_fusion.1
  207.4 5.3 copy.107
  212.7 6.6 %all-to-all-start.1 = ((f32[2,2,512,512]{2,1,0,3:T(2,128)}), f32[2,2,512,512]{2,1,0,3:T(2,128)}, u32[]{:S(2)}, u32[]{:S(2)}) async-start(f32[2,2,512,512]{2,1,0,3:T(2,128)} %copy.107), calls=%async_computation.1 | async-start | bytes 8388608 | tf_op jit(solution)/shard_map/all_to_all | solution.py:104
  219.8 92.8 %all-to-all-done.1 = f32[2,2,512,512]{2,1,0,3:T(2,128)} async-done(((f32[2,2,512,512]{2,1,0,3:T(2,128)}), f32[2,2,512,512]{2,1,0,3:T(2,128)}, u32[]{:S(2)}, u32[]{:S(2)}) %all-to-all-start.1) | async-done | bytes 4194336 | tf_op jit(solution)/shard_map/all_to_all | solution.py:104
  312.7 3.7 fusion.264
  317.1 3.4 fusion.12
  320.5 3.4 fusion.10
  323.9 3.8 fusion.30
  327.6 4.2 fusion
  331.9 3.2 fusion.4
  335.0 3.2 fusion.2
  338.3 3.6 subtract_bitcast_fusion
  341.9 3.4 add_bitcast_fusion
  350.0 1.9 fusion.62
  351.9 1.4 fusion.60
  353.3 1.4 fusion.43
  354.7 1.4 fusion.42
  357.5 1.6 copy.128
  359.1 57.4 %all_to_all.21 = f32[2,2,256,512]{2,1,0,3:T(2,128)S(1)} all-to-all(f32[2,2,256,512]{2,1,0,3:T(2,128)S(1)} %copy.128), channel_id=1, replica_groups=mesh['grp'=4,'pos'=64] {'pos'}, dimensions={3} | all-to-all | bytes 4194304 | tf_op jit(solution)/shard_map/all_to_all | solution.py:139
  417.4 1.4 fusion.56
  418.8 1.4 fusion.54
  420.4 1.4 fusion.41
  422.4 1.4 fusion.40
  424.6 3.0 copy.137
  427.6 6.7 %all-to-all-start.3 = ((f32[2,2,256,512]{2,1,0,3:T(2,128)}), f32[2,2,256,512]{2,1,0,3:T(2,128)S(1)}, u32[]{:S(2)}, u32[]{:S(2)}) async-start(f32[2,2,256,512]{2,1,0,3:T(2,128)} %copy.137), calls=%async_computation.3 | async-start | bytes 4194304 | tf_op jit(solution)/shard_map/all_to_all | solution.py:144
  434.5 48.8 %all-to-all-done.3 = f32[2,2,256,512]{2,1,0,3:T(2,128)S(1)} async-done(((f32[2,2,256,512]{2,1,0,3:T(2,128)}), f32[2,2,256,512]{2,1,0,3:T(2,128)S(1)}, u32[]{:S(2)}, u32[]{:S(2)}) %all-to-all-start.3) | async-done | bytes 2097184 | tf_op jit(solution)/shard_map/all_to_all | solution.py:144
  483.3 2.0 fusion.267
  485.4 2.4 copy.154
  487.7 1.6 copy.155
  489.3 1.9 multiply_subtract_fusion.5
  491.2 1.5 pad_maximum_fusion.7
  492.9 4.3 collective-permute-done.2
  497.2 2.1 subtract_select_fusion.2
  500.1 5.0 collective-permute-start.3
  505.1 24.3 %collective-permute-done.3 = f32[1,256,512]{2,1,0:T(8,128)S(1)} collective-permute-done((f32[1,256,512]{2,1,0:T(8,128)S(1)}, f32[1,256,512]{2,1,0:T(8,128)S(1)}, u32[]{:S(2)}, u32[]{:S(2)}) %collective-permute-start.3) | collective-permute-done | bytes 524320 | tf_op jit(solution)/shard_map/ppermute | solution.py:18
  (57 shorter events, 20.3 us)
Async XLA Ops:
  0.0 11.1 %copy-start.2 = (f32[256,512]{1,0:T(8,128)S(1)}, f32[256,512]{1,0:T(8,128)}, u32[]{:S(2)}) copy-start(f32[256,512]{1,0:T(8,128)} %param.8) | copy-start | bytes 1572868
  3.6 51.9 %collective-permute-start = (f32[512,512]{1,0:T(8,128)}, f32[512,512]{1,0:T(8,128)S(1)}, u32[]{:S(2)}, u32[]{:S(2)}) collective-permute-start(f32[512,512]{1,0:T(8,128)} %get-tuple-element.33), channel_id=1, source_target_pairs={{0,128},{128,0},{64,192},{192,64},{1,129},{129,1},{65,193},{193,65... | collective-permute-start | bytes 3145736 | tf_op jit(solution)/shard_map/ppermute | solution.py:18
  57.9 2.6 copy-start
  60.6 7.5 %collective-permute-start.1 = (f32[2,2,512,512]{3,2,1,0:T(8,128)}, f32[2,2,512,512]{3,2,1,0:T(8,128)}, u32[]{:S(2)}, u32[]{:S(2)}) collective-permute-start(f32[2,2,512,512]{3,2,1,0:T(8,128)} %pad_maximum_fusion.2), channel_id=1, source_target_pairs={{0,64},{64,0},{128,192},{192,128},{1,65},{65,1},{129,193},{193,129... | collective-permute-start | bytes 12582920 | tf_op jit(solution)/shard_map/ppermute | solution.py:18
  212.7 100.0 %all-to-all-start.1 = ((f32[2,2,512,512]{2,1,0,3:T(2,128)}), f32[2,2,512,512]{2,1,0,3:T(2,128)}, u32[]{:S(2)}, u32[]{:S(2)}) async-start(f32[2,2,512,512]{2,1,0,3:T(2,128)} %copy.107), calls=%async_computation.1 | async-start | bytes 8388608 | tf_op jit(solution)/shard_map/all_to_all | solution.py:104
  427.6 55.7 %all-to-all-start.3 = ((f32[2,2,256,512]{2,1,0,3:T(2,128)}), f32[2,2,256,512]{2,1,0,3:T(2,128)S(1)}, u32[]{:S(2)}, u32[]{:S(2)}) async-start(f32[2,2,256,512]{2,1,0,3:T(2,128)} %copy.137), calls=%async_computation.3 | async-start | bytes 4194304 | tf_op jit(solution)/shard_map/all_to_all | solution.py:144
  485.4 2.4 copy-start.1
  492.7 4.5 collective-permute-start.2
  499.8 29.6 %copy-start.3 = (f32[256,512]{1,0:T(8,128)S(1)}, f32[256,512]{1,0:T(8,128)}, u32[]{:S(2)}) copy-start(f32[256,512]{1,0:T(8,128)} %param.5) | copy-start | bytes 1572868
  499.8 29.6 %copy-start.4 = (f32[256]{0:T(256)S(1)}, f32[256]{0:T(256)}, u32[]{:S(2)}) copy-start(f32[256]{0:T(256)} %param.9) | copy-start | bytes 3076
  500.1 29.4 %collective-permute-start.3 = (f32[1,256,512]{2,1,0:T(8,128)S(1)}, f32[1,256,512]{2,1,0:T(8,128)S(1)}, u32[]{:S(2)}, u32[]{:S(2)}) collective-permute-start(f32[1,256,512]{2,1,0:T(8,128)S(1)} %multiply_subtract_fusion.9), channel_id=1, source_target_pairs={{0,128},{128,0},{64,192},{192,64},{1,129},{129,1},{65,193},{193,65... | collective-permute-start | bytes 1572872 | tf_op jit(solution)/shard_map/ppermute | solution.py:18
where the time goes:
time: 537 us; the launch traced here: 531 us
  waiting for transfers between devices  221 us (41%)
  blocking collectives  163 us (30%)
  matrix products  58.7 us (11%)
  local copies, waits for them, and re-layouts  34.5 us (6%)
  other arithmetic  26.4 us (5%)
  starting transfers between devices  25.5 us (5%)
    all_to_all x2, waiting for transfers between devices, body(): lax.all_to_all(mixed_line.reshape(2, 2, row_count, line_width), 'pos', sp...  142 us
    all_to_all x1, blocking collectives, body(): lax.all_to_all(spectra, 'pos', split_axis=3, concat_axis=3, tiled=True)  106 us
    ppermute x4, waiting for transfers between devices, from_partner(): return lax.ppermute(block, axis, route)  79.6 us
    all_to_all x1, blocking collectives, body(): lax.all_to_all(product, 'pos', split_axis=3, concat_axis=3, tiled=True)  57.4 us
    dot_general x6, matrix products, dft_apply(): jnp.einsum(pattern, cos_part, values[0], precision=precise)  15.5 us
    dot_general x6, matrix products, dft_apply(): jnp.einsum(pattern, sin_part, values[0], precision=precise)  15.1 us
    dot_general x6, matrix products, dft_apply(): jnp.einsum(pattern, cos_part, values[1], precision=precise)  14.2 us
    dot_general x6, matrix products, dft_apply(): jnp.einsum(pattern, sin_part, values[1], precision=precise)  13.9 us
  transfers between devices with their start and end apart: 6, of which 6 were waited for; matrix products, arithmetic and copies ran while one was open for 0% of the time, Pallas kernels for 0%

commit v1 on v0

v1 whole, which is shorter than its diff:
```python
import numpy as np

import jax
import jax.numpy as jnp
from jax import lax
from jax.sharding import PartitionSpec as P

AXES = ("grp", "pos")


def turns(numerator, denominator):
    angle = 2.0 * np.pi * (numerator % denominator) / denominator
    return np.cos(angle), np.sin(angle)


def tables(lines, width):
    length = lines * width
    line = np.arange(lines)
    offset = np.arange(width)
    c1, s1 = turns(np.outer(4 * line + 1, line), 4 * lines)
    ct, st = turns(np.outer(4 * line + 1, offset), 4 * length)
    c2, s2 = turns(np.outer(offset, offset), width)
    first = np.concatenate([c1, -s1], 0)
    second = np.block([[c2, -s2], [s2, c2]])
    back_second = np.block([[c2, s2], [-s2, c2]]) / length
    back_first = np.concatenate([c1.T, -s1.T], 1)
    return [a.astype(np.float32) for a in (first, ct, st, second, back_second, back_first)]


def dot(a, b):
    return jnp.dot(a, b, precision=lax.Precision.HIGH, preferred_element_type=jnp.float32)


def body(query, key_branch, value_branch, long_filter, skip_gain):
    channels, width = query.shape
    lines = lax.axis_size("grp") * lax.axis_size("pos")
    first, ct, st, second, back_second, back_first = tables(lines, width)
    gated = key_branch * value_branch
    both = jnp.concatenate(
        [gated.reshape(channels, width // 128, 128), long_filter.reshape(channels, width // 128, 128)], 1
    )
    both = lax.all_to_all(both, AXES, split_axis=0, concat_axis=0, tiled=True)
    both = both.reshape(lines, 2 * width)
    spread = dot(first, both)
    real, imag = spread[:lines], spread[lines:]
    cc, ss = jnp.tile(ct, (1, 2)), jnp.tile(st, (1, 2))
    real, imag = real * cc + imag * ss, imag * cc - real * ss
    rows = jnp.concatenate([real, imag], 1)
    rows = rows.reshape(lines, 2, 2, width).transpose(2, 0, 1, 3).reshape(2 * lines, 2 * width)
    spectra = dot(rows, second)
    ar, ai = spectra[:lines, :width], spectra[:lines, width:]
    br, bi = spectra[lines:, :width], spectra[lines:, width:]
    product = jnp.concatenate([ar * br - ai * bi, ar * bi + ai * br], 1)
    back = dot(product, back_second)
    real, imag = back[:, :width], back[:, width:]
    real, imag = real * ct - imag * st, imag * ct + real * st
    convolved = dot(back_first, jnp.concatenate([real, imag], 0))
    convolved = lax.all_to_all(
        convolved.reshape(lines, width // 128, 128), AXES, split_axis=0, concat_axis=0, tiled=True
    ).reshape(channels, width)
    return query * (convolved + skip_gain[:, None] * gated)


def solution(mesh):
    return jax.shard_map(
        body,
        mesh=mesh,
        in_specs=(P(None, AXES), P(None, AXES), P(None, AXES), P(None, AXES), P()),
        out_specs=P(None, AXES),
        check_vma=False,
    )
```

time: 537 us -> 95.6 us (0.18)
  waiting for transfers between devices: 221 us -> 27.9 us
  blocking collectives: 163 us -> 25.7 us
  matrix products: 58.7 us -> 9.65 us
  local copies, waits for them, and re-layouts: 34.5 us -> 12 us
  other arithmetic: 26.4 us -> 4.13 us
  starting transfers between devices: 25.5 us -> 14.5 us
    all_to_all x2 -> x1, blocking collectives: 163 us -> 25.7 us  [body(): lax.all_to_all(convolved.reshape(lines, width // 128, 128), AXES, split_a...]
    all_to_all x2 -> x1, waiting for transfers between devices: 142 us -> 27.9 us  [body(): both = lax.all_to_all(both, AXES, split_axis=0, concat_axis=0, tiled=True)]
    ppermute x4 -> x0, waiting for transfers between devices: 79.6 us -> none  [from_partner(): return lax.ppermute(block, axis, route)]
    dot_general x24 -> x6, matrix products: 58.7 us -> 9.65 us  [dot(): jnp.dot(a, b, precision=lax.Precision.HIGH, preferred_element_type=jnp.fl...]
    another operation x6 -> x2, local copies, waits for them, and re-layouts: 17.7 us -> 0.72 us  [body(): cc, ss = (jnp.tile(ct, (1, 2)), jnp.tile(st, (1, 2)))]
    ppermute x4 -> x0, starting transfers between devices: 12.2 us -> none  [from_partner(): return lax.ppermute(block, axis, route)]
    another operation x10 -> x0, other arithmetic: 10.2 us -> none  [the longest x4 6.69 us: rotate_by(): jnp.stack([values[0] * cos_part - values[1] * sin_part, values[0] * sin_p...]
    slice x4 -> x0, local copies, waits for them, and re-layouts: 7.84 us -> none  [the longest x1 3.66 us: rotate_by(): values[1] * sin_part]
  transfers between devices with their start and end apart: 6 -> 1, of which waited for: 6 -> 1; matrix products, arithmetic and copies ran while one was open for 0% -> 3% of each run, Pallas kernels for 0% -> 0%
where the time goes in v1:
time: 95.6 us; the launch traced here: 94.2 us
  waiting for transfers between devices  27.9 us (29%)
  blocking collectives  25.7 us (27%)
  starting transfers between devices  14.5 us (15%)
  local copies, waits for them, and re-layouts  12 us (13%)
  matrix products  9.65 us (10%)
  other arithmetic  4.13 us (4%)
    all_to_all x1, waiting for transfers between devices, body(): both = lax.all_to_all(both, AXES, split_axis=0, concat_axis=0, tiled=True)  27.9 us
    all_to_all x1, blocking collectives, body(): lax.all_to_all(convolved.reshape(lines, width // 128, 128), AXES, split_a...  25.7 us
    all_to_all x1, starting transfers between devices, body(): both = lax.all_to_all(both, AXES, split_axis=0, concat_axis=0, tiled=True)  14.5 us
    dot_general x6, matrix products, dot(): jnp.dot(a, b, precision=lax.Precision.HIGH, preferred_element_type=jnp.fl...  9.65 us
    reshape x2, local copies, waits for them, and re-layouts, body(): rows.reshape(lines, 2, 2, width).transpose(2, 0, 1, 3)  5.47 us
    unnamed x29, local copies, waits for them, and re-layouts  5.27 us
  transfers between devices with their start and end apart: 1, of which 1 were waited for; matrix products, arithmetic and copies ran while one was open for 3% of the time, Pallas kernels for 0%

profile of v1, /device:TPU:16, one launch (start us, length us, event | category | flops | bytes accessed | tf_op | source)
XLA Modules:
  0.0 94.2 jit_solution(15955041134924412520)
XLA Ops:
  0.0 0.0 copy-start.8
  0.0 1.3 %mul.50 = f32[256,512]{1,0:T(8,128)S(1)} multiply(f32[256,512]{1,0:T(8,128)} %param.14, f32[256,512]{1,0:T(8,128)} %param.15) | non-fusion elementwise | flops 131072 | bytes 1572864 | tf_op jit(solution)/shard_map/mul | solution.py:38
  1.3 0.2 reshape.30
  1.5 0.0 copy-done.8
  1.5 0.2 reshape.31
  1.7 0.0 copy-start
  1.7 1.2 %pad_maximum_fusion.1 = f32[256,8,128]{2,1,0:T(8,128)} fusion(f32[256,4,128]{2,1,0:T(4,128)S(1)} %reshape.31, f32[256,4,128]{2,1,0:T(4,128)S(1)} %reshape.30), kind=kLoop, calls=%fused_computation.6 | loop fusion | flops 262144 | bytes 2097152 | tf_op jit(solution)/shard_map/concatenate | solution.py:39
  2.9 14.5 %all-to-all-start = ((f32[256,8,128]{2,1,0:T(8,128)}), f32[256,8,128]{2,1,0:T(8,128)S(1)}, u32[]{:S(2)}, u32[]{:S(2)}) async-start(f32[256,8,128]{2,1,0:T(8,128)} %pad_maximum_fusion.1), calls=%async_computation | async-start | bytes 2097152 | tf_op jit(solution)/shard_map/all_to_all | solution.py:42
  17.4 0.0 copy-done
  17.4 0.0 copy-start.1
  17.5 0.4 tile.8
  17.8 1.2 %copy.20 = f32[32,8,2,512]{3,1,2,0:T(8,128)} copy(f32[32,8,2,512]{3,2,1,0:T(2,128)S(1)} %bitcast.30) | data formatting | bytes 2097152
  19.0 0.0 copy-done.1
  19.0 0.4 tile.20
  19.4 1.2 %copy.21 = f32[32,8,2,512]{3,1,2,0:T(8,128)} copy(f32[32,8,2,512]{3,2,1,0:T(2,128)S(1)} %bitcast.31) | data formatting | bytes 2097152
  20.6 0.0 copy-start.4
  20.6 27.9 %all-to-all-done = f32[256,8,128]{2,1,0:T(8,128)S(1)} async-done(((f32[256,8,128]{2,1,0:T(8,128)}), f32[256,8,128]{2,1,0:T(8,128)S(1)}, u32[]{:S(2)}, u32[]{:S(2)}) %all-to-all-start) | async-done | bytes 1048608 | tf_op jit(solution)/shard_map/all_to_all | solution.py:42
  48.4 0.0 copy-start.5
  48.4 2.2 %fusion = f32[512,1024]{1,0:T(8,128)S(1)} fusion(f32[512,256]{1,0:T(8,128)} %constant.12.clone, f32[32,8,8,128]{3,2,1,0:T(8,128)S(1)} %bitcast.29), kind=kOutput, calls=%fused_computation.3 | convolution fusion | flops 805306368 | bytes 3670016 | tf_op jit(solution)/shard_map/dot_general | solution.py:31
  50.7 0.0 copy-done.4
  50.7 0.0 copy-done.5
  50.7 0.5 multiply_add_fusion
  51.2 0.1 pad_maximum_fusion
  51.4 2.8 %reshape.33 = f32[256,2,2,512]{3,2,1,0:T(2,128)} reshape(f32[256,2048]{1,0:T(8,128)S(1)} %pad_maximum_fusion) | data formatting | bytes 4194304 | tf_op jit(solution)/shard_map/reshape | solution.py:49
  54.2 2.7 %copy.17 = f32[256,2,2,512]{3,1,0,2:T(2,128)S(1)} copy(f32[256,2,2,512]{3,2,1,0:T(2,128)} %reshape.33) | data formatting | bytes 4194304 | tf_op jit(solution)/shard_map/reshape | solution.py:49
  56.9 0.0 copy-start.3
  56.9 0.5 copy.22
  57.3 1.7 %copy-done.3 = f32[1024,1024]{1,0:T(8,128)S(1)} copy-done((f32[1024,1024]{1,0:T(8,128)S(1)}, f32[1024,1024]{1,0:T(8,128)}, u32[]{:S(2)}) %copy-start.3) | copy-done | bytes 4194328
  59.0 0.0 copy-start.6
  59.0 3.8 %fusion.30 = f32[512,1024]{1,0:T(8,128)S(1)} fusion(f32[512,1024]{1,0:T(8,128)S(1)} %bitcast.28, f32[1024,1024]{1,0:T(8,128)S(1)} %copy-done.3), kind=kOutput, calls=%fused_computation.37 | convolution fusion | flops 3221225472 | bytes 8388608 | tf_op jit(solution)/shard_map/dot_general | solution.py:31
  62.8 0.0 copy-done.6
  62.8 0.0 copy-start.7
  62.8 1.2 %fusion.14 = f32[256,1024]{1,0:T(8,128)S(1)} fusion(f32[512,1024]{1,0:T(8,128)S(1)} %copy-done.6, f32[512,1024]{1,0:T(8,128)S(1)} %fusion.30), kind=kOutput, calls=%fused_computation.21 | convolution fusion | flops 805699584 | bytes 5242880 | tf_op jit(solution)/shard_map/dot_general | solution.py:31
  64.0 0.4 copy-done.7
  64.4 0.0 copy-start.2
  64.4 0.0 copy-start.10
  64.4 1.2 %convolution_add_fusion = f32[256,1024]{1,0:T(8,128)S(1)} fusion(f32[256,1024]{1,0:T(8,128)S(1)} %fusion.14, f32[512,1024]{1,0:T(8,128)S(1)} %copy-done.7, f32[512,1024]{1,0:T(8,128)S(1)} %fusion.30), kind=kOutput, calls=%fused_computation.1 | convolution fusion | flops 805961728 | bytes 6291456 | tf_op jit(solution)/shard_map/dot_general | solution.py:31
  65.6 0.0 copy-done.2
  65.7 0.0 copy-done.10
  65.7 0.0 copy-start.11
  65.7 0.6 fusion.7
  66.3 0.3 copy-done.11
  66.6 0.6 convolution_add_fusion.1
  67.3 0.2 copy.18
  67.5 25.7 %all_to_all.10 = f32[256,4,128]{2,1,0:T(4,128)S(1)} all-to-all(f32[256,4,128]{2,1,0:T(4,128)S(1)} %copy.18), channel_id=1, replica_groups=mesh['grp'=4,'pos'=64] {'grp','pos'}, dimensions={0} | all-to-all | bytes 1048576 | tf_op jit(solution)/shard_map/all_to_all | solution.py:58
  93.2 0.0 copy-done.9
  93.2 0.0 copy-done.12
  93.2 0.9 fusion.3
  (2 shorter events, 0.0 us)
Async XLA Ops:
  0.0 1.5 %copy-start.8 = (f32[256,512]{1,0:T(8,128)S(1)}, f32[256,512]{1,0:T(8,128)}, u32[]{:S(2)}) copy-start(f32[256,512]{1,0:T(8,128)} %param.16) | copy-start | bytes 1572868
  1.7 15.7 %copy-start = (f32[256,512]{1,0:T(8,128)S(1)}, f32[256,512]{1,0:T(8,128)}, u32[]{:S(2)}) copy-start(f32[256,512]{1,0:T(8,128)} %constant.13.clone) | copy-start | bytes 1572868
  2.9 45.5 %all-to-all-start = ((f32[256,8,128]{2,1,0:T(8,128)}), f32[256,8,128]{2,1,0:T(8,128)S(1)}, u32[]{:S(2)}, u32[]{:S(2)}) async-start(f32[256,8,128]{2,1,0:T(8,128)} %pad_maximum_fusion.1), calls=%async_computation | async-start | bytes 2097152 | tf_op jit(solution)/shard_map/all_to_all | solution.py:42
  17.4 1.6 %copy-start.1 = (f32[256,512]{1,0:T(8,128)S(1)}, f32[256,512]{1,0:T(8,128)}, u32[]{:S(2)}) copy-start(f32[256,512]{1,0:T(8,128)} %constant.14.clone) | copy-start | bytes 1572868
  20.6 30.1 %copy-start.4 = (f32[32,8,2,512]{3,1,2,0:T(8,128)S(1)}, f32[32,8,2,512]{3,1,2,0:T(8,128)}, u32[]{:S(2)}) copy-start(f32[32,8,2,512]{3,1,2,0:T(8,128)} %copy.20) | copy-start | bytes 3145732
  48.4 2.2 %copy-start.5 = (f32[32,8,2,512]{3,1,2,0:T(8,128)S(1)}, f32[32,8,2,512]{3,1,2,0:T(8,128)}, u32[]{:S(2)}) copy-start(f32[32,8,2,512]{3,1,2,0:T(8,128)} %copy.21) | copy-start | bytes 3145732
  56.9 2.2 %copy-start.3 = (f32[1024,1024]{1,0:T(8,128)S(1)}, f32[1024,1024]{1,0:T(8,128)}, u32[]{:S(2)}) copy-start(f32[1024,1024]{1,0:T(8,128)} %constant.15.clone) | copy-start | bytes 12582916
  59.0 3.8 %copy-start.6 = (f32[512,1024]{1,0:T(8,128)S(1)}, f32[512,1024]{1,0:T(8,128)}, u32[]{:S(2)}) copy-start(f32[512,1024]{1,0:T(8,128)} %constant.18) | copy-start | bytes 6291460
  62.8 1.6 %copy-start.7 = (f32[512,1024]{1,0:T(8,128)S(1)}, f32[512,1024]{1,0:T(8,128)}, u32[]{:S(2)}) copy-start(f32[512,1024]{1,0:T(8,128)} %constant.19) | copy-start | bytes 6291460
  64.4 1.2 %copy-start.2 = (f32[256,512]{1,0:T(8,128)S(1)}, f32[256,512]{1,0:T(8,128)}, u32[]{:S(2)}) copy-start(f32[256,512]{1,0:T(8,128)} %constant.14.clone) | copy-start | bytes 1572868
  64.4 1.2 %copy-start.10 = (f32[256,256]{1,0:T(8,128)S(1)}, f32[256,256]{1,0:T(8,128)}, u32[]{:S(2)}) copy-start(f32[256,256]{1,0:T(8,128)} %constant.20) | copy-start | bytes 786436
  65.7 1.0 %copy-start.11 = (f32[256,256]{1,0:T(8,128)S(1)}, f32[256,256]{1,0:T(8,128)}, u32[]{:S(2)}) copy-start(f32[256,256]{1,0:T(8,128)} %constant.21) | copy-start | bytes 786436
  66.6 26.6 %copy-start.9 = (f32[256,512]{1,0:T(8,128)S(1)}, f32[256,512]{1,0:T(8,128)}, u32[]{:S(2)}) copy-start(f32[256,512]{1,0:T(8,128)} %param.13) | copy-start | bytes 1572868
  66.6 26.6 %copy-start.12 = (f32[256]{0:T(256)S(1)}, f32[256]{0:T(256)}, u32[]{:S(2)}) copy-start(f32[256]{0:T(256)} %param.17) | copy-start | bytes 3076

commit v2 on v1

v2 whole, which is shorter than its diff:
```python
import functools

import ml_dtypes
import numpy as np

import jax
import jax.numpy as jnp
from jax import lax
from jax.experimental import pallas as pl
from jax.experimental.pallas import tpu as pltpu
from jax.sharding import PartitionSpec as P

AXES = ("grp", "pos")
LANES = 128
RADIX = 4
PARAMS = pltpu.CompilerParams(vmem_limit_bytes=40 * 2**20)


def turns(numerator, denominator):
    angle = 2.0 * np.pi * (numerator % denominator) / denominator
    return np.cos(angle), np.sin(angle)


def high_low(table):
    high = table.astype(ml_dtypes.bfloat16)
    low = (table - high.astype(np.float64)).astype(ml_dtypes.bfloat16)
    return high, low


def left_table(table):
    high, low = high_low(table)
    return np.concatenate([high, low, high], -1)


def right_table(table):
    high, low = high_low(table)
    return np.concatenate([high, low, high], -2)


@functools.lru_cache
def tables(lines, width):
    length = lines * width
    line = np.arange(lines)
    offset = np.arange(width)
    c1, s1 = turns(np.outer(4 * line + 1, line), 4 * lines)
    ct, st = turns(np.outer(4 * line + 1, offset), 4 * length)
    small = np.arange(width // RADIX)
    forth, back = [], []
    for r in range(RADIX):
        c2, s2 = turns(np.outer(small, RADIX * small + r), width)
        block = np.block([[c2, -s2], [s2, c2]])
        forth.append(block)
        back.append(block.T / length)
    return (
        left_table(np.concatenate([c1, -s1], 0)),
        np.concatenate([ct, st], 0).astype(np.float32),
        right_table(np.stack(forth)),
        right_table(np.stack(back)),
        left_table(np.concatenate([c1.T, -s1.T], 1)),
    )


def split(x):
    high = x.astype(jnp.bfloat16)
    return high, (x - high.astype(jnp.float32)).astype(jnp.bfloat16)


def dot(a, b):
    return jnp.dot(a, b, preferred_element_type=jnp.float32)


def gate_kernel(key_ref, value_ref, filter_ref, out_ref):
    channels, width = key_ref.shape
    blocks = width // LANES
    for q in range(blocks):
        at = pl.ds(q * LANES, LANES)
        out_ref[pl.ds(q, channels, stride=2 * blocks), :] = key_ref[:, at] * value_ref[:, at]
        out_ref[pl.ds(blocks + q, channels, stride=2 * blocks), :] = filter_ref[:, at]


def convolve_kernel(x_ref, first_ref, twist_ref, forth_ref, back_ref, last_ref, y_ref, xs, a, zh, zl, c, dh, dl):
    lines = y_ref.shape[0] // RADIX
    width = RADIX * LANES
    step = 32
    for j in range(2 * RADIX):
        high, low = split(x_ref[pl.ds(j, lines, stride=2 * RADIX), :])
        at = pl.ds(j * LANES, LANES)
        xs[0:lines, at] = high
        xs[lines : 2 * lines, at] = high
        xs[2 * lines : 3 * lines, at] = low
    for n in range(0, 2 * width, 256):
        a[:, n : n + 256] = dot(first_ref[...], xs[:, n : n + 256])
    for signal in range(2):
        for row in range(0, lines, step):
            re, im = [], []
            for q in range(RADIX):
                at = slice(signal * width + q * LANES, signal * width + (q + 1) * LANES)
                ar, ai = a[row : row + step, at], a[lines + row : lines + row + step, at]
                at = slice(q * LANES, (q + 1) * LANES)
                ct, st = twist_ref[row : row + step, at], twist_ref[lines + row : lines + row + step, at]
                re.append(ar * ct + ai * st)
                im.append(ai * ct - ar * st)
            e0r, e0i, e1r, e1i = re[0] + re[2], im[0] + im[2], re[0] - re[2], im[0] - im[2]
            o0r, o0i, o1r, o1i = re[1] + re[3], im[1] + im[3], re[1] - re[3], im[1] - im[3]
            outs = (
                (e0r + o0r, e0i + o0i),
                (e1r + o1i, e1i - o1r),
                (e0r - o0r, e0i - o0i),
                (e1r - o1i, e1i + o1r),
            )
            rows = slice(signal * lines + row, signal * lines + row + step)
            for r, pair in enumerate(outs):
                for part, value in enumerate(pair):
                    high, low = split(value)
                    at = slice(part * LANES, (part + 1) * LANES)
                    zh[r, rows, at] = high
                    zl[r, rows, at] = low
    for r in range(RADIX):
        high = zh[r]
        spectra = dot(jnp.concatenate([high, high, zl[r]], 1), forth_ref[r])
        gr, gi = spectra[:lines, :LANES], spectra[:lines, LANES:]
        fr, fi = spectra[lines:, :LANES], spectra[lines:, LANES:]
        high, low = split(jnp.concatenate([gr * fr - gi * fi, gr * fi + gi * fr], 1))
        c[r] = dot(jnp.concatenate([high, high, low], 1), back_ref[r])
    for row in range(0, lines, step):
        re = [c[r, row : row + step, :LANES] for r in range(RADIX)]
        im = [c[r, row : row + step, LANES:] for r in range(RADIX)]
        e0r, e0i, e1r, e1i = re[0] + re[2], im[0] + im[2], re[0] - re[2], im[0] - im[2]
        o0r, o0i, o1r, o1i = re[1] + re[3], im[1] + im[3], re[1] - re[3], im[1] - im[3]
        outs = (
            (e0r + o0r, e0i + o0i),
            (e1r - o1i, e1i + o1r),
            (e0r - o0r, e0i - o0i),
            (e1r + o1i, e1i - o1r),
        )
        for q, (dr, di) in enumerate(outs):
            at = slice(q * LANES, (q + 1) * LANES)
            ct, st = twist_ref[row : row + step, at], twist_ref[lines + row : lines + row + step, at]
            for part, value in enumerate((dr * ct - di * st, di * ct + dr * st)):
                high, low = split(value)
                rows = slice(part * lines + row, part * lines + row + step)
                dh[rows, at] = high
                dl[rows, at] = low
    for q in range(0, RADIX, 2):
        at = slice(q * LANES, (q + 2) * LANES)
        high = dh[:, at]
        y = dot(last_ref[...], jnp.concatenate([high, high, dl[:, at]], 0))
        y_ref[pl.ds(q, lines, stride=RADIX), :] = y[:, :LANES]
        y_ref[pl.ds(q + 1, lines, stride=RADIX), :] = y[:, LANES:]


def mix_kernel(query_ref, key_ref, value_ref, skip_ref, y_ref, out_ref):
    channels, width = query_ref.shape
    blocks = width // LANES
    skip = skip_ref[...]
    for q in range(blocks):
        at = pl.ds(q * LANES, LANES)
        y = y_ref[pl.ds(q, channels, stride=blocks), :]
        out_ref[:, at] = query_ref[:, at] * (y + skip * (key_ref[:, at] * value_ref[:, at]))


def convolve(x, lines, width):
    return pl.pallas_call(
        convolve_kernel,
        out_shape=jax.ShapeDtypeStruct((lines * RADIX, LANES), jnp.float32),
        scratch_shapes=[
            pltpu.VMEM((3 * lines, 2 * width), jnp.bfloat16),
            pltpu.VMEM((2 * lines, 2 * width), jnp.float32),
            pltpu.VMEM((RADIX, 2 * lines, 2 * LANES), jnp.bfloat16),
            pltpu.VMEM((RADIX, 2 * lines, 2 * LANES), jnp.bfloat16),
            pltpu.VMEM((RADIX, lines, 2 * LANES), jnp.float32),
            pltpu.VMEM((2 * lines, width), jnp.bfloat16),
            pltpu.VMEM((2 * lines, width), jnp.bfloat16),
        ],
        compiler_params=PARAMS,
    )(x, *tables(lines, width))


def body(query, key_branch, value_branch, long_filter, skip_gain):
    channels, width = query.shape
    lines = lax.axis_size("grp") * lax.axis_size("pos")
    blocks = width // LANES
    both = pl.pallas_call(
        gate_kernel,
        out_shape=jax.ShapeDtypeStruct((channels * 2 * blocks, LANES), jnp.float32),
        compiler_params=PARAMS,
    )(key_branch, value_branch, long_filter)
    both = lax.all_to_all(
        both.reshape(channels, 2 * blocks, LANES), AXES, split_axis=0, concat_axis=0, tiled=True
    )
    y = convolve(both.reshape(lines * 2 * blocks, LANES), lines, width)
    y = lax.all_to_all(y.reshape(lines, blocks, LANES), AXES, split_axis=0, concat_axis=0, tiled=True)
    return pl.pallas_call(
        mix_kernel,
        out_shape=jax.ShapeDtypeStruct((channels, width), jnp.float32),
        compiler_params=PARAMS,
    )(query, key_branch, value_branch, skip_gain.reshape(channels, 1), y.reshape(channels * blocks, LANES))


def solution(mesh):
    return jax.shard_map(
        body,
        mesh=mesh,
        in_specs=(P(None, AXES), P(None, AXES), P(None, AXES), P(None, AXES), P()),
        out_specs=P(None, AXES),
        check_vma=False,
    )
```

time: 95.6 us -> 85.5 us (0.89)
  blocking collectives: 25.7 us -> 45.3 us
  matrix products: 9.65 us -> 0 us
  starting transfers between devices: 14.5 us -> 6.08 us
  waiting for transfers between devices: 27.9 us -> 19.7 us
  Pallas kernels: 0 us -> 7.34 us
  local copies, waits for them, and re-layouts: 12 us -> 5.55 us
  other arithmetic: 4.13 us -> 0 us
    all_to_all x1, blocking collectives: 25.7 us -> 45.3 us  [body(): lax.all_to_all(both.reshape(channels, 2 * blocks, LANES), AXES, split_axi...]
    dot_general x6 -> x0, matrix products: 9.65 us -> none  [dot(): jnp.dot(a, b, precision=lax.Precision.HIGH, preferred_element_type=jnp.fl...]
    all_to_all x1, starting transfers between devices: 14.5 us -> 6.08 us  [body(): lax.all_to_all(y.reshape(lines, blocks, LANES), AXES, split_axis=0, conca...]
    all_to_all x1, waiting for transfers between devices: 27.9 us -> 19.7 us  [body(): lax.all_to_all(y.reshape(lines, blocks, LANES), AXES, split_axis=0, conca...]
    pallas_call x0 -> x3, Pallas kernels: none -> 7.34 us  [the longest x1 6.13 us: convolve(): pl.pallas_call(convolve_kernel, out_shape=jax.ShapeDtypeStruct((lines * R...]
    reshape x5 -> x1, local copies, waits for them, and re-layouts: 6.06 us -> 0.13 us  [body(): skip_gain.reshape(channels, 1)]
    mul x2 -> x0, other arithmetic: 2.27 us -> none  [the longest x1 1.34 us: body(): gated = key_branch * value_branch]
    concatenate x2 -> x0, other arithmetic: 1.33 us -> none  [the longest x1 1.19 us: body(): jnp.concatenate([gated.reshape(channels, width // 128, 128), long_filter....]
  transfers between devices with their start and end apart: 1 -> 1, of which waited for: 1 -> 1; matrix products, arithmetic and copies ran while one was open for 3% -> 0% of each run, Pallas kernels for 0% -> 0%
where the time goes in v2:
time: 85.5 us; the launch traced here: 84 us
  blocking collectives  45.3 us (53%)
  waiting for transfers between devices  19.7 us (23%)
  Pallas kernels  7.34 us (9%)
  starting transfers between devices  6.08 us (7%)
  local copies, waits for them, and re-layouts  5.55 us (6%)
    all_to_all x1, blocking collectives, body(): lax.all_to_all(both.reshape(channels, 2 * blocks, LANES), AXES, split_axi...  45.3 us
    all_to_all x1, waiting for transfers between devices, body(): lax.all_to_all(y.reshape(lines, blocks, LANES), AXES, split_axis=0, conca...  19.7 us
    pallas_call x1, Pallas kernels, convolve(): pl.pallas_call(convolve_kernel, out_shape=jax.ShapeDtypeStruct((lines * R...  6.13 us
    all_to_all x1, starting transfers between devices, body(): lax.all_to_all(y.reshape(lines, blocks, LANES), AXES, split_axis=0, conca...  6.08 us
    unnamed x24, local copies, waits for them, and re-layouts  5.41 us
  transfers between devices with their start and end apart: 1, of which 1 were waited for; matrix products, arithmetic and copies ran while one was open for 0% of the time, Pallas kernels for 0%

profile of v2, /device:TPU:16, one launch (start us, length us, event | category | flops | bytes accessed | tf_op | source)
XLA Modules:
  0.0 84.0 jit_solution(5339805272613898300)
XLA Ops:
  0.0 0.0 copy-start
  0.0 1.0 %copy-done = f32[256,512]{1,0:T(8,128)S(1)} copy-done((f32[256,512]{1,0:T(8,128)S(1)}, f32[256,512]{1,0:T(8,128)}, u32[]{:S(2)}) %copy-start) | copy-done | bytes 524312
  1.0 0.0 copy-start.2
  1.0 1.0 %copy-done.2 = f32[256,512]{1,0:T(8,128)S(1)} copy-done((f32[256,512]{1,0:T(8,128)S(1)}, f32[256,512]{1,0:T(8,128)}, u32[]{:S(2)}) %copy-start.2) | copy-done | bytes 524312
  2.1 0.0 copy-start.9
  2.1 1.0 %copy-done.9 = f32[256,512]{1,0:T(8,128)S(1)} copy-done((f32[256,512]{1,0:T(8,128)S(1)}, f32[256,512]{1,0:T(8,128)}, u32[]{:S(2)}) %copy-start.9) | copy-done | bytes 524312
  3.1 0.0 copy-start.5
  3.1 0.0 copy-start.6
  3.1 0.3 shard_map.100
  3.4 0.0 copy-start.4
  3.4 45.3 %all_to_all.10 = f32[256,8,128]{2,1,0:T(8,128)S(1)} all-to-all(f32[256,8,128]{2,1,0:T(8,128)S(1)} %bitcast.6), channel_id=1, replica_groups=mesh['grp'=4,'pos'=64] {'grp','pos'}, dimensions={0} | all-to-all | bytes 2097152 | tf_op jit(solution)/shard_map/all_to_all | solution.py:188
  48.7 0.0 copy-done.5
  48.7 0.0 copy-done.6
  48.7 0.0 copy-done.4
  48.7 0.0 copy-start.7
  48.8 1.1 %copy-done.7 = bf16[512,768]{1,0:T(8,128)(2,1)S(1)} copy-done((bf16[512,768]{1,0:T(8,128)(2,1)S(1)}, bf16[512,768]{1,0:T(8,128)(2,1)}, u32[]{:S(2)}) %copy-start.7) | copy-done | bytes 786456
  49.9 0.0 copy-start.8
  49.9 1.1 %copy-done.8 = bf16[256,1536]{1,0:T(8,128)(2,1)S(1)} copy-done((bf16[256,1536]{1,0:T(8,128)(2,1)S(1)}, bf16[256,1536]{1,0:T(8,128)(2,1)}, u32[]{:S(2)}) %copy-start.8) | copy-done | bytes 786456
  51.0 0.0 copy-start.11
  51.0 0.0 copy-start.1
  51.0 0.0 copy-start.3
  51.0 0.0 copy-start.10
  51.0 6.1 %shard_map.101 = f32[1024,128]{1,0:T(8,128)} custom-call(f32[2048,128]{1,0:T(8,128)S(1)} %bitcast.5, bf16[512,768]{1,0:T(8,128)(2,1)S(1)} %copy-done.7, f32[512,512]{1,0:T(8,128)S(1)} %copy-done.6, bf16[4,768,256]{2,1,0:T(8,128)(2,1)S(1)} %copy-done.4, bf16[4,768,256]{2,1,0:T(8,128)(2,1)S(1)} %copy-done.5, bf16[256,1536]{1,0:T(8,128)(2,1)S(1)} %copy-done.8), custom_call_target="tpu_custom_call" | custom-call | tf_op jit(solution)/shard_map/pallas_call | solution.py:163
  57.2 6.1 %all-to-all-start.1 = ((f32[256,4,128]{2,1,0:T(4,128)}), f32[256,4,128]{2,1,0:T(4,128)S(1)}, u32[]{:S(2)}, u32[]{:S(2)}) async-start(f32[256,4,128]{2,1,0:T(4,128)} %bitcast.3), calls=%async_computation.1 | async-start | bytes 1048576 | tf_op jit(solution)/shard_map/all_to_all | solution.py:192
  63.2 0.0 copy-done.11
  63.3 0.1 copy.11.skip_ref
  63.4 19.7 %all-to-all-done.1 = f32[256,4,128]{2,1,0:T(4,128)S(1)} async-done(((f32[256,4,128]{2,1,0:T(4,128)}), f32[256,4,128]{2,1,0:T(4,128)S(1)}, u32[]{:S(2)}, u32[]{:S(2)}) %all-to-all-start.1) | async-done | bytes 524320 | tf_op jit(solution)/shard_map/all_to_all | solution.py:192
  83.1 0.0 copy-done.1
  83.1 0.0 copy-done.3
  83.1 0.0 copy-done.10
  83.1 0.9 %shard_map.102 = f32[256,512]{1,0:T(8,128)} custom-call(f32[256,512]{1,0:T(8,128)S(1)} %copy-done.10, f32[256,512]{1,0:T(8,128)S(1)} %copy-done.1, f32[256,512]{1,0:T(8,128)S(1)} %copy-done.3, f32[256,1]{1,0:T(8,128)S(1)} %copy.11.skip_ref, f32[1024,128]{1,0:T(8,128)S(1)} %bitcast.7), custom_call_target="tpu_custom_call" | custom-call | tf_op jit(solution)/shard_map/pallas_call | solution.py:193
Async XLA Ops:
  0.0 1.0 %copy-start = (f32[256,512]{1,0:T(8,128)S(1)}, f32[256,512]{1,0:T(8,128)}, u32[]{:S(2)}) copy-start(f32[256,512]{1,0:T(8,128)} %key_ref.3) | copy-start | bytes 1572868
  1.0 1.0 %copy-start.2 = (f32[256,512]{1,0:T(8,128)S(1)}, f32[256,512]{1,0:T(8,128)}, u32[]{:S(2)}) copy-start(f32[256,512]{1,0:T(8,128)} %value_ref.3) | copy-start | bytes 1572868
  2.1 1.0 %copy-start.9 = (f32[256,512]{1,0:T(8,128)S(1)}, f32[256,512]{1,0:T(8,128)}, u32[]{:S(2)}) copy-start(f32[256,512]{1,0:T(8,128)} %filter_ref.1) | copy-start | bytes 1572868
  3.1 45.6 %copy-start.5 = (bf16[4,768,256]{2,1,0:T(8,128)(2,1)S(1)}, bf16[4,768,256]{2,1,0:T(8,128)(2,1)}, u32[]{:S(2)}) copy-start(bf16[4,768,256]{2,1,0:T(8,128)(2,1)} %constant.13.clone.back_ref) | copy-start | bytes 4718596
  3.1 45.6 %copy-start.6 = (f32[512,512]{1,0:T(8,128)S(1)}, f32[512,512]{1,0:T(8,128)}, u32[]{:S(2)}) copy-start(f32[512,512]{1,0:T(8,128)} %constant.11.clone.twist_ref) | copy-start | bytes 3145732
  3.4 45.3 %copy-start.4 = (bf16[4,768,256]{2,1,0:T(8,128)(2,1)S(1)}, bf16[4,768,256]{2,1,0:T(8,128)(2,1)}, u32[]{:S(2)}) copy-start(bf16[4,768,256]{2,1,0:T(8,128)(2,1)} %constant.12.clone.forth_ref) | copy-start | bytes 4718596
  48.7 1.1 %copy-start.7 = (bf16[512,768]{1,0:T(8,128)(2,1)S(1)}, bf16[512,768]{1,0:T(8,128)(2,1)}, u32[]{:S(2)}) copy-start(bf16[512,768]{1,0:T(8,128)(2,1)} %constant.10.clone.first_ref) | copy-start | bytes 2359300
  49.9 1.1 %copy-start.8 = (bf16[256,1536]{1,0:T(8,128)(2,1)S(1)}, bf16[256,1536]{1,0:T(8,128)(2,1)}, u32[]{:S(2)}) copy-start(bf16[256,1536]{1,0:T(8,128)(2,1)} %constant.14.clone.last_ref) | copy-start | bytes 2359300
  51.0 12.2 %copy-start.11 = (f32[256]{0:T(256)S(1)}, f32[256]{0:T(256)}, u32[]{:S(2)}) copy-start(f32[256]{0:T(256)} %param.14) | copy-start | bytes 3076
  51.0 32.1 %copy-start.1 = (f32[256,512]{1,0:T(8,128)S(1)}, f32[256,512]{1,0:T(8,128)}, u32[]{:S(2)}) copy-start(f32[256,512]{1,0:T(8,128)} %key_ref.3) | copy-start | bytes 1572868
  51.0 32.1 %copy-start.3 = (f32[256,512]{1,0:T(8,128)S(1)}, f32[256,512]{1,0:T(8,128)}, u32[]{:S(2)}) copy-start(f32[256,512]{1,0:T(8,128)} %value_ref.3) | copy-start | bytes 1572868
  51.0 32.1 %copy-start.10 = (f32[256,512]{1,0:T(8,128)S(1)}, f32[256,512]{1,0:T(8,128)}, u32[]{:S(2)}) copy-start(f32[256,512]{1,0:T(8,128)} %query_ref.1) | copy-start | bytes 1572868
  57.2 25.9 %all-to-all-start.1 = ((f32[256,4,128]{2,1,0:T(4,128)}), f32[256,4,128]{2,1,0:T(4,128)S(1)}, u32[]{:S(2)}, u32[]{:S(2)}) async-start(f32[256,4,128]{2,1,0:T(4,128)} %bitcast.3), calls=%async_computation.1 | async-start | bytes 1048576 | tf_op jit(solution)/shard_map/all_to_all | solution.py:192

commit v3 on v2

v3 whole, which is shorter than its diff:
```python
import functools

import ml_dtypes
import numpy as np

import jax
import jax.numpy as jnp
from jax import lax
from jax.experimental import pallas as pl
from jax.experimental.pallas import tpu as pltpu
from jax.sharding import PartitionSpec as P

AXES = ("grp", "pos")
LANES = 128
RADIX = 4
CHUNKS = 2
ROW_PARTS = 1


def params(mib):
    return pltpu.CompilerParams(vmem_limit_bytes=mib * 2**20)


def turns(numerator, denominator):
    angle = 2.0 * np.pi * (numerator % denominator) / denominator
    return np.cos(angle), np.sin(angle)


def high_low(table):
    high = table.astype(ml_dtypes.bfloat16)
    low = (table - high.astype(np.float64)).astype(ml_dtypes.bfloat16)
    return high, low


def table_pair(table, axis):
    return np.concatenate(high_low(table), axis)


@functools.lru_cache
def tables(lines, width):
    length = lines * width
    line = np.arange(lines)
    offset = np.arange(width)
    c1, s1 = turns(np.outer(4 * line + 1, line), 4 * lines)
    ct, st = turns(np.outer(4 * line + 1, offset), 4 * length)
    small = np.arange(width // RADIX)
    forth, back = [], []
    for r in range(RADIX):
        c2, s2 = turns(np.outer(small, RADIX * small + r), width)
        block = np.block([[c2, -s2], [s2, c2]])
        forth.append(block)
        back.append(block.T / length)
    spread = np.concatenate([c1.reshape(ROW_PARTS, -1, lines), -s1.reshape(ROW_PARTS, -1, lines)], 1)
    return (
        table_pair(spread, -1),
        np.concatenate([ct, st], 0).astype(np.float32),
        table_pair(np.stack(forth), -2),
        table_pair(np.stack(back), -2),
        table_pair(np.concatenate([c1.T, -s1.T], 1), -1),
    )


def split(x):
    high = x.astype(jnp.bfloat16)
    return high, (x - high.astype(jnp.float32)).astype(jnp.bfloat16)


def dot(a, b):
    return jnp.dot(a, b, preferred_element_type=jnp.float32)


def dot_left(table, high, low):
    depth = high.shape[0]
    table = jnp.concatenate([table, table[:, :depth]], 1)
    return dot(table, jnp.concatenate([high, high, low], 0))


def dot_right(high, low, table):
    depth = high.shape[1]
    table = jnp.concatenate([table, table[:depth]], 0)
    return dot(jnp.concatenate([high, high, low], 1), table)


def gate_kernel(key_hbm, value_hbm, filter_hbm, skip_hbm, out_ref, key_ref, value_ref, filter_ref, skip_ref, sems):
    channels, width = key_ref.shape
    blocks = width // LANES
    part = channels // CHUNKS

    def copies(i):
        rows = pl.ds(i * part, part)
        pairs = ((key_hbm, key_ref), (value_hbm, value_ref), (filter_hbm, filter_ref))
        return [
            pltpu.make_async_copy(there.at[rows], here.at[rows], sems.at[n, i]) for n, (there, here) in enumerate(pairs)
        ]

    skip_copy = pltpu.make_async_copy(skip_hbm, skip_ref, sems.at[3, 0])
    skip_copy.start()
    for i in range(CHUNKS):
        for copy in copies(i):
            copy.start()
    first_device = (lax.axis_index(AXES[0]) == 0) & (lax.axis_index(AXES[1]) == 0)
    lane = lax.broadcasted_iota(jnp.int32, (part, LANES), 1)
    first_position = (lane == 0) & first_device
    skip_copy.wait()
    for i in range(CHUNKS):
        for copy in copies(i):
            copy.wait()
        rows = pl.ds(i * part, part)
        skip = jnp.broadcast_to(skip_ref[:, i * part : (i + 1) * part], (LANES, part)).T
        skip = jnp.where(first_position, skip, 0.0)
        for q in range(blocks):
            at = pl.ds(q * LANES, LANES)
            first = i * part * 2 * blocks + q
            lags = filter_ref[rows, at]
            out_ref[pl.ds(first, part, stride=2 * blocks), :] = key_ref[rows, at] * value_ref[rows, at]
            out_ref[pl.ds(first + blocks, part, stride=2 * blocks), :] = lags + skip if q == 0 else lags


def four(pairs, sign):
    (ar, ai), (br, bi), (cr, ci), (dr, di) = pairs
    e0r, e0i, e1r, e1i = ar + cr, ai + ci, ar - cr, ai - ci
    o0r, o0i, o1r, o1i = br + dr, bi + di, br - dr, bi - di
    turned, other = (e1r - o1i, e1i + o1r), (e1r + o1i, e1i - o1r)
    if sign < 0:
        turned, other = other, turned
    return (e0r + o0r, e0i + o0i), turned, (e0r - o0r, e0i - o0i), other


def convolve_kernel(x_ref, first_ref, twist_ref, forth_ref, back_ref, last_ref, y_ref, xh, xl, zh, zl, dh, dl):
    lines = y_ref.shape[0] // RADIX
    width = RADIX * LANES
    count = first_ref.shape[0]
    rows = lines // count
    for j in range(2 * RADIX):
        high, low = split(x_ref[pl.ds(j, lines, stride=2 * RADIX), :])
        at = pl.ds(j * LANES, LANES)
        xh[:, at] = high
        xl[:, at] = low
    for i in range(count):
        here, there = slice(i * rows, (i + 1) * rows), slice(lines + i * rows, lines + (i + 1) * rows)
        twist = [
            (twist_ref[here, q * LANES : (q + 1) * LANES], twist_ref[there, q * LANES : (q + 1) * LANES])
            for q in range(RADIX)
        ]
        for signal in range(2):
            at = slice(signal * width, (signal + 1) * width)
            spread = dot_left(first_ref[i], xh[:, at], xl[:, at])
            pairs = []
            for q, (ct, st) in enumerate(twist):
                at = slice(q * LANES, (q + 1) * LANES)
                re, im = spread[:rows, at], spread[rows:, at]
                pairs.append((re * ct + im * st, im * ct - re * st))
            at = slice(signal * rows, (signal + 1) * rows)
            for r, pair in enumerate(four(pairs, -1)):
                for part, value in enumerate(pair):
                    high, low = split(value)
                    zh[i, r, at, part * LANES : (part + 1) * LANES] = high
                    zl[i, r, at, part * LANES : (part + 1) * LANES] = low
        pairs = []
        for r in range(RADIX):
            spectra = dot_right(zh[i, r], zl[i, r], forth_ref[r])
            gr, gi = spectra[:rows, :LANES], spectra[:rows, LANES:]
            fr, fi = spectra[rows:, :LANES], spectra[rows:, LANES:]
            high, low = split(jnp.concatenate([gr * fr - gi * fi, gr * fi + gi * fr], 1))
            back = dot_right(high, low, back_ref[r])
            pairs.append((back[:, :LANES], back[:, LANES:]))
        for q, (re, im) in enumerate(four(pairs, 1)):
            ct, st = twist[q]
            at = slice(q * LANES, (q + 1) * LANES)
            dh[here, at], dl[here, at] = split(re * ct - im * st)
            dh[there, at], dl[there, at] = split(im * ct + re * st)
    for q in range(0, RADIX, 2):
        at = slice(q * LANES, (q + 2) * LANES)
        y = dot_left(last_ref[...], dh[:, at], dl[:, at])
        y_ref[pl.ds(q, lines, stride=RADIX), :] = y[:, :LANES]
        y_ref[pl.ds(q + 1, lines, stride=RADIX), :] = y[:, LANES:]


def mix_kernel(query_ref, y_ref, out_hbm, out_ref, sems):
    channels, width = query_ref.shape
    blocks = width // LANES
    part = channels // CHUNKS
    copies = []
    for i in range(CHUNKS):
        rows = pl.ds(i * part, part)
        for q in range(blocks):
            at = pl.ds(q * LANES, LANES)
            out_ref[rows, at] = query_ref[rows, at] * y_ref[pl.ds(i * part * blocks + q, part, stride=blocks), :]
        copies.append(pltpu.make_async_copy(out_ref.at[rows], out_hbm.at[rows], sems.at[i]))
        copies[-1].start()
    for copy in copies:
        copy.wait()


def convolve(x, lines, width):
    return pl.pallas_call(
        convolve_kernel,
        out_shape=jax.ShapeDtypeStruct((lines * RADIX, LANES), jnp.float32),
        scratch_shapes=[
            pltpu.VMEM((lines, 2 * width), jnp.bfloat16),
            pltpu.VMEM((lines, 2 * width), jnp.bfloat16),
            pltpu.VMEM((ROW_PARTS, RADIX, 2 * lines // ROW_PARTS, 2 * LANES), jnp.bfloat16),
            pltpu.VMEM((ROW_PARTS, RADIX, 2 * lines // ROW_PARTS, 2 * LANES), jnp.bfloat16),
            pltpu.VMEM((2 * lines, width), jnp.bfloat16),
            pltpu.VMEM((2 * lines, width), jnp.bfloat16),
        ],
        compiler_params=params(32),
    )(x, *tables(lines, width))


def body(query, key_branch, value_branch, long_filter, skip_gain):
    channels, width = query.shape
    lines = lax.axis_size("grp") * lax.axis_size("pos")
    blocks = width // LANES
    sources = [
        pltpu.with_memory_space_constraint(x, pltpu.HBM)
        for x in (key_branch, value_branch, long_filter, skip_gain.reshape(1, channels))
    ]
    both = pl.pallas_call(
        gate_kernel,
        out_shape=pltpu.VMEM((channels * 2 * blocks, LANES), jnp.float32),
        in_specs=[pl.BlockSpec(memory_space=pltpu.HBM)] * 4,
        scratch_shapes=[
            pltpu.VMEM((channels, width), jnp.float32),
            pltpu.VMEM((channels, width), jnp.float32),
            pltpu.VMEM((channels, width), jnp.float32),
            pltpu.VMEM((1, channels), jnp.float32),
            pltpu.SemaphoreType.DMA((4, CHUNKS)),
        ],
        compiler_params=params(16),
    )(*sources)
    both = lax.all_to_all(
        both.reshape(channels, 2 * blocks, LANES), AXES, split_axis=0, concat_axis=0, tiled=True
    )
    y = convolve(both.reshape(lines * 2 * blocks, LANES), lines, width)
    y = lax.all_to_all(y.reshape(lines, blocks, LANES), AXES, split_axis=0, concat_axis=0, tiled=True)
    return pl.pallas_call(
        mix_kernel,
        out_shape=jax.ShapeDtypeStruct((channels, width), jnp.float32),
        out_specs=pl.BlockSpec(memory_space=pltpu.HBM),
        scratch_shapes=[pltpu.VMEM((channels, width), jnp.float32), pltpu.SemaphoreType.DMA((CHUNKS,))],
        compiler_params=params(16),
    )(query, y.reshape(channels * blocks, LANES))


def solution(mesh):
    return jax.shard_map(
        body,
        mesh=mesh,
        in_specs=(P(None, AXES), P(None, AXES), P(None, AXES), P(None, AXES), P()),
        out_specs=P(None, AXES),
        check_vma=False,
    )
```

time: 85.5 us -> 80.2 us (0.938)
  blocking collectives: 45.3 us -> 71 us
  waiting for transfers between devices: 19.7 us -> 0 us
  starting transfers between devices: 6.08 us -> 0 us
  local copies, waits for them, and re-layouts: 5.55 us -> 0.03 us
    all_to_all x0 -> x1, blocking collectives: none -> 25.7 us  [body(): lax.all_to_all(y.reshape(lines, blocks, LANES), AXES, split_axis=0, conca...]
    all_to_all x1 -> x0, waiting for transfers between devices: 19.7 us -> none  [body(): lax.all_to_all(y.reshape(lines, blocks, LANES), AXES, split_axis=0, conca...]
    all_to_all x1 -> x0, starting transfers between devices: 6.08 us -> none  [body(): lax.all_to_all(y.reshape(lines, blocks, LANES), AXES, split_axis=0, conca...]
    unnamed x24 -> x12, local copies, waits for them, and re-layouts: 5.41 us -> 0.03 us
    pallas_call x1, Pallas kernels: 0.27 us -> 1.78 us  [body(): pl.pallas_call(gate_kernel, out_shape=pltpu.VMEM((channels * 2 * blocks,...]
    pallas_call x1, Pallas kernels: 6.13 us -> 5.24 us  [convolve(): pl.pallas_call(convolve_kernel, out_shape=jax.ShapeDtypeStruct((lines * R...]
  transfers between devices with their start and end apart: 1 -> 0, of which waited for: 1 -> 0; matrix products, arithmetic and copies ran while one was open for 0% -> 0% of each run, Pallas kernels for 0% -> 0%
where the time goes in v3:
time: 80.2 us; the launch traced here: 79 us
  blocking collectives  71 us (89%)
  Pallas kernels  7.86 us (10%)
    all_to_all x1, blocking collectives, body(): lax.all_to_all(both.reshape(channels, 2 * blocks, LANES), AXES, split_axi...  45.3 us
    all_to_all x1, blocking collectives, body(): lax.all_to_all(y.reshape(lines, blocks, LANES), AXES, split_axis=0, conca...  25.7 us
    pallas_call x1, Pallas kernels, convolve(): pl.pallas_call(convolve_kernel, out_shape=jax.ShapeDtypeStruct((lines * R...  5.24 us
    pallas_call x1, Pallas kernels, body(): pl.pallas_call(gate_kernel, out_shape=pltpu.VMEM((channels * 2 * blocks,...  1.78 us

profile of v3, /device:TPU:16, one launch (start us, length us, event | category | flops | bytes accessed | tf_op | source)
XLA Modules:
  0.0 79.0 jit_solution(9340014941723841138)
XLA Ops:
  0.0 0.0 copy-start.2
  0.0 0.0 copy-start.4
  0.0 0.0 copy-start.5
  0.0 1.8 %shard_map.100 = f32[2048,128]{1,0:T(8,128)S(1)} custom-call(f32[256,512]{1,0:T(8,128)} %key_hbm.1, f32[256,512]{1,0:T(8,128)} %value_hbm.1, f32[256,512]{1,0:T(8,128)} %filter_hbm.1, f32[1,256]{1,0:T(1,128)} %bitcast.9), custom_call_target="tpu_custom_call" | custom-call | tf_op jit(solution)/shard_map/pallas_call | solution.py:219
  1.8 0.0 copy-start
  1.8 0.0 copy-start.1
  1.8 45.3 %all_to_all.10 = f32[256,8,128]{2,1,0:T(8,128)S(1)} all-to-all(f32[256,8,128]{2,1,0:T(8,128)S(1)} %bitcast.5), channel_id=1, replica_groups=mesh['grp'=4,'pos'=64] {'grp','pos'}, dimensions={0} | all-to-all | bytes 2097152 | tf_op jit(solution)/shard_map/all_to_all | solution.py:232
  47.1 0.0 copy-done.2
  47.1 0.0 copy-done.4
  47.1 0.0 copy-done.5
  47.1 0.0 copy-done
  47.2 0.0 copy-done.1
  47.2 5.2 %shard_map.101 = f32[1024,128]{1,0:T(8,128)S(1)} custom-call(f32[2048,128]{1,0:T(8,128)S(1)} %bitcast.6, bf16[1,512,512]{2,1,0:T(8,128)(2,1)S(1)} %copy-done.5, f32[512,512]{1,0:T(8,128)S(1)} %copy-done.2, bf16[4,512,256]{2,1,0:T(8,128)(2,1)S(1)} %copy-done.1, bf16[4,512,256]{2,1,0:T(8,128)(2,1)S(1)} %copy-done, bf16[256,1024]{1,0:T(8,128)(2,1)S(1)} %copy-done.4), custom_call_target="tpu_custom_call" | custom-call | tf_op jit(solution)/shard_map/pallas_call | solution.py:196
  52.4 0.0 copy-start.3
  52.4 25.7 %all_to_all.11 = f32[256,4,128]{2,1,0:T(4,128)S(1)} all-to-all(f32[256,4,128]{2,1,0:T(4,128)S(1)} %bitcast.8), channel_id=1, replica_groups=mesh['grp'=4,'pos'=64] {'grp','pos'}, dimensions={0} | all-to-all | bytes 1048576 | tf_op jit(solution)/shard_map/all_to_all | solution.py:236
  78.1 0.0 copy-done.3
  78.1 0.8 %shard_map.102 = f32[256,512]{1,0:T(8,128)} custom-call(f32[256,512]{1,0:T(8,128)S(1)} %copy-done.3, f32[1024,128]{1,0:T(8,128)S(1)} %bitcast.7), custom_call_target="tpu_custom_call" | custom-call | tf_op jit(solution)/shard_map/pallas_call | solution.py:237
Async XLA Ops:
  0.0 47.1 %copy-start.2 = (f32[512,512]{1,0:T(8,128)S(1)}, f32[512,512]{1,0:T(8,128)}, u32[]{:S(2)}) copy-start(f32[512,512]{1,0:T(8,128)} %constant.11.clone.twist_ref) | copy-start | bytes 3145732
  0.0 47.1 %copy-start.4 = (bf16[256,1024]{1,0:T(8,128)(2,1)S(1)}, bf16[256,1024]{1,0:T(8,128)(2,1)}, u32[]{:S(2)}) copy-start(bf16[256,1024]{1,0:T(8,128)(2,1)} %constant.14.clone.last_ref) | copy-start | bytes 1572868
  0.0 47.1 %copy-start.5 = (bf16[1,512,512]{2,1,0:T(8,128)(2,1)S(1)}, bf16[1,512,512]{2,1,0:T(8,128)(2,1)}, u32[]{:S(2)}) copy-start(bf16[1,512,512]{2,1,0:T(8,128)(2,1)} %constant.10.clone.first_ref) | copy-start | bytes 1572868
  1.8 45.3 %copy-start = (bf16[4,512,256]{2,1,0:T(8,128)(2,1)S(1)}, bf16[4,512,256]{2,1,0:T(8,128)(2,1)}, u32[]{:S(2)}) copy-start(bf16[4,512,256]{2,1,0:T(8,128)(2,1)} %constant.13.clone.back_ref) | copy-start | bytes 3145732
  1.8 45.3 %copy-start.1 = (bf16[4,512,256]{2,1,0:T(8,128)(2,1)S(1)}, bf16[4,512,256]{2,1,0:T(8,128)(2,1)}, u32[]{:S(2)}) copy-start(bf16[4,512,256]{2,1,0:T(8,128)(2,1)} %constant.12.clone.forth_ref) | copy-start | bytes 3145732
  52.4 25.7 %copy-start.3 = (f32[256,512]{1,0:T(8,128)S(1)}, f32[256,512]{1,0:T(8,128)}, u32[]{:S(2)}) copy-start(f32[256,512]{1,0:T(8,128)} %query_ref.1) | copy-start | bytes 1572868

commit v4 on v3

--- a/solution.py
+++ b/solution.py
@@ -14,7 +14,7 @@
 LANES = 128
 RADIX = 4
 CHUNKS = 2
-ROW_PARTS = 1
+STEP = 32
 
 
 def params(mib):
@@ -50,9 +50,8 @@
         block = np.block([[c2, -s2], [s2, c2]])
         forth.append(block)
         back.append(block.T / length)
-    spread = np.concatenate([c1.reshape(ROW_PARTS, -1, lines), -s1.reshape(ROW_PARTS, -1, lines)], 1)
     return (
-        table_pair(spread, -1),
+        table_pair(np.concatenate([c1, -s1], 0), -1),
         np.concatenate([ct, st], 0).astype(np.float32),
         table_pair(np.stack(forth), -2),
         table_pair(np.stack(back), -2),
@@ -129,46 +128,66 @@
 def convolve_kernel(x_ref, first_ref, twist_ref, forth_ref, back_ref, last_ref, y_ref, xh, xl, zh, zl, dh, dl):
     lines = y_ref.shape[0] // RADIX
     width = RADIX * LANES
-    count = first_ref.shape[0]
-    rows = lines // count
-    for j in range(2 * RADIX):
-        high, low = split(x_ref[pl.ds(j, lines, stride=2 * RADIX), :])
-        at = pl.ds(j * LANES, LANES)
-        xh[:, at] = high
-        xl[:, at] = low
-    for i in range(count):
-        here, there = slice(i * rows, (i + 1) * rows), slice(lines + i * rows, lines + (i + 1) * rows)
-        twist = [
-            (twist_ref[here, q * LANES : (q + 1) * LANES], twist_ref[there, q * LANES : (q + 1) * LANES])
-            for q in range(RADIX)
-        ]
-        for signal in range(2):
-            at = slice(signal * width, (signal + 1) * width)
-            spread = dot_left(first_ref[i], xh[:, at], xl[:, at])
+    lower, upper = slice(0, lines), slice(lines, 2 * lines)
+
+    def lanes(q):
+        return slice(q * LANES, (q + 1) * LANES)
+
+    def take(signal):
+        for q in range(RADIX):
+            j = signal * RADIX + q
+            xh[:, lanes(j)], xl[:, lanes(j)] = split(x_ref[pl.ds(j, lines, stride=2 * RADIX), :])
+
+    def over_lines(signal):
+        at = slice(signal * width, (signal + 1) * width)
+        return dot_left(first_ref[...], xh[:, at], xl[:, at])
+
+    def turn(signal, spread):
+        at = slice(signal * lines, (signal + 1) * lines)
+        for row in range(0, lines, STEP):
+            rows = slice(row, row + STEP)
+            below = slice(lines + row, lines + row + STEP)
+            here = slice(signal * lines + row, signal * lines + row + STEP)
             pairs = []
-            for q, (ct, st) in enumerate(twist):
-                at = slice(q * LANES, (q + 1) * LANES)
-                re, im = spread[:rows, at], spread[rows:, at]
+            for q in range(RADIX):
+                re, im = spread[rows, lanes(q)], spread[below, lanes(q)]
+                ct, st = twist_ref[rows, lanes(q)], twist_ref[below, lanes(q)]
                 pairs.append((re * ct + im * st, im * ct - re * st))
-            at = slice(signal * rows, (signal + 1) * rows)
             for r, pair in enumerate(four(pairs, -1)):
                 for part, value in enumerate(pair):
-                    high, low = split(value)
-                    zh[i, r, at, part * LANES : (part + 1) * LANES] = high
-                    zl[i, r, at, part * LANES : (part + 1) * LANES] = low
-        pairs = []
-        for r in range(RADIX):
-            spectra = dot_right(zh[i, r], zl[i, r], forth_ref[r])
-            gr, gi = spectra[:rows, :LANES], spectra[:rows, LANES:]
-            fr, fi = spectra[rows:, :LANES], spectra[rows:, LANES:]
-            high, low = split(jnp.concatenate([gr * fr - gi * fi, gr * fi + gi * fr], 1))
-            back = dot_right(high, low, back_ref[r])
-            pairs.append((back[:, :LANES], back[:, LANES:]))
-        for q, (re, im) in enumerate(four(pairs, 1)):
-            ct, st = twist[q]
-            at = slice(q * LANES, (q + 1) * LANES)
-            dh[here, at], dl[here, at] = split(re * ct - im * st)
-            dh[there, at], dl[there, at] = split(im * ct + re * st)
+                    zh[r, here, lanes(part)], zl[r, here, lanes(part)] = split(value)
+
+    def over_offsets(signal, r):
+        at = slice(signal * lines, (signal + 1) * lines)
+        return dot_right(zh[r, at], zl[r, at], forth_ref[r])
+
+    def product(g, f):
+        gr, gi, fr, fi = g[:, :LANES], g[:, LANES:], f[:, :LANES], f[:, LANES:]
+        return split(jnp.concatenate([gr * fr - gi * fi, gr * fi + gi * fr], 1))
+
+    def turn_back(backs):
+        for row in range(0, lines, STEP):
+            rows = slice(row, row + STEP)
+            below = slice(lines + row, lines + row + STEP)
+            pairs = [(back[rows, :LANES], back[rows, LANES:]) for back in backs]
+            for q, (re, im) in enumerate(four(pairs, 1)):
+                ct, st = twist_ref[rows, lanes(q)], twist_ref[below, lanes(q)]
+                dh[rows, lanes(q)], dl[rows, lanes(q)] = split(re * ct - im * st)
+                dh[below, lanes(q)], dl[below, lanes(q)] = split(im * ct + re * st)
+
+    take(0)
+    spread_g = over_lines(0)
+    take(1)
+    spread_f = over_lines(1)
+    turn(0, spread_g)
+    gs = [over_offsets(0, r) for r in range(RADIX)]
+    turn(1, spread_f)
+    fs = [over_offsets(1, r) for r in range(RADIX)]
+    backs = []
+    for r in range(RADIX):
+        high, low = product(gs[r], fs[r])
+        backs.append(dot_right(high, low, back_ref[r]))
+    turn_back(backs)
     for q in range(0, RADIX, 2):
         at = slice(q * LANES, (q + 2) * LANES)
         y = dot_left(last_ref[...], dh[:, at], dl[:, at])
@@ -199,8 +218,8 @@
         scratch_shapes=[
             pltpu.VMEM((lines, 2 * width), jnp.bfloat16),
             pltpu.VMEM((lines, 2 * width), jnp.bfloat16),
-            pltpu.VMEM((ROW_PARTS, RADIX, 2 * lines // ROW_PARTS, 2 * LANES), jnp.bfloat16),
-            pltpu.VMEM((ROW_PARTS, RADIX, 2 * lines // ROW_PARTS, 2 * LANES), jnp.bfloat16),
+            pltpu.VMEM((RADIX, 2 * lines, 2 * LANES), jnp.bfloat16),
+            pltpu.VMEM((RADIX, 2 * lines, 2 * LANES), jnp.bfloat16),
             pltpu.VMEM((2 * lines, width), jnp.bfloat16),
             pltpu.VMEM((2 * lines, width), jnp.bfloat16),
         ],

time: 80.2 us -> 78.7 us (0.981)
  Pallas kernels: 7.86 us -> 6.38 us
    pallas_call x1, Pallas kernels: 5.24 us -> 3.76 us  [convolve(): pl.pallas_call(convolve_kernel, out_shape=jax.ShapeDtypeStruct((lines * R...]
where the time goes in v4:
time: 78.7 us; the launch traced here: 77.5 us
  blocking collectives  71 us (90%)
  Pallas kernels  6.38 us (8%)
    all_to_all x1, blocking collectives, body(): lax.all_to_all(both.reshape(channels, 2 * blocks, LANES), AXES, split_axi...  45.3 us
    all_to_all x1, blocking collectives, body(): lax.all_to_all(y.reshape(lines, blocks, LANES), AXES, split_axis=0, conca...  25.7 us
    pallas_call x1, Pallas kernels, convolve(): pl.pallas_call(convolve_kernel, out_shape=jax.ShapeDtypeStruct((lines * R...  3.76 us
    pallas_call x1, Pallas kernels, body(): pl.pallas_call(gate_kernel, out_shape=pltpu.VMEM((channels * 2 * blocks,...  1.78 us

profile of v4, /device:TPU:16, one launch (start us, length us, event | category | flops | bytes accessed | tf_op | source)
XLA Modules:
  0.0 77.5 jit_solution(6020770757133160354)
XLA Ops:
  0.0 0.0 copy-start.2
  0.0 0.0 copy-start.4
  0.0 0.0 copy-start.5
  0.0 1.8 %shard_map.100 = f32[2048,128]{1,0:T(8,128)S(1)} custom-call(f32[256,512]{1,0:T(8,128)} %key_hbm.1, f32[256,512]{1,0:T(8,128)} %value_hbm.1, f32[256,512]{1,0:T(8,128)} %filter_hbm.1, f32[1,256]{1,0:T(1,128)} %bitcast.9), custom_call_target="tpu_custom_call" | custom-call | tf_op jit(solution)/shard_map/pallas_call | solution.py:238
  1.8 0.0 copy-start
  1.8 0.0 copy-start.1
  1.8 45.3 %all_to_all.10 = f32[256,8,128]{2,1,0:T(8,128)S(1)} all-to-all(f32[256,8,128]{2,1,0:T(8,128)S(1)} %bitcast.5), channel_id=1, replica_groups=mesh['grp'=4,'pos'=64] {'grp','pos'}, dimensions={0} | all-to-all | bytes 2097152 | tf_op jit(solution)/shard_map/all_to_all | solution.py:251
  47.1 0.0 copy-done.2
  47.1 0.0 copy-done.4
  47.1 0.0 copy-done.5
  47.1 0.0 copy-done
  47.2 0.0 copy-done.1
  47.2 3.8 %shard_map.101 = f32[1024,128]{1,0:T(8,128)S(1)} custom-call(f32[2048,128]{1,0:T(8,128)S(1)} %bitcast.6, bf16[512,512]{1,0:T(8,128)(2,1)S(1)} %copy-done.5, f32[512,512]{1,0:T(8,128)S(1)} %copy-done.2, bf16[4,512,256]{2,1,0:T(8,128)(2,1)S(1)} %copy-done.1, bf16[4,512,256]{2,1,0:T(8,128)(2,1)S(1)} %copy-done, bf16[256,1024]{1,0:T(8,128)(2,1)S(1)} %copy-done.4), custom_call_target="tpu_custom_call" | custom-call | tf_op jit(solution)/shard_map/pallas_call | solution.py:215
  50.9 0.0 copy-start.3
  50.9 25.7 %all_to_all.11 = f32[256,4,128]{2,1,0:T(4,128)S(1)} all-to-all(f32[256,4,128]{2,1,0:T(4,128)S(1)} %bitcast.8), channel_id=1, replica_groups=mesh['grp'=4,'pos'=64] {'grp','pos'}, dimensions={0} | all-to-all | bytes 1048576 | tf_op jit(solution)/shard_map/all_to_all | solution.py:255
  76.7 0.0 copy-done.3
  76.7 0.8 %shard_map.102 = f32[256,512]{1,0:T(8,128)} custom-call(f32[256,512]{1,0:T(8,128)S(1)} %copy-done.3, f32[1024,128]{1,0:T(8,128)S(1)} %bitcast.7), custom_call_target="tpu_custom_call" | custom-call | tf_op jit(solution)/shard_map/pallas_call | solution.py:256
Async XLA Ops:
  0.0 47.1 %copy-start.2 = (f32[512,512]{1,0:T(8,128)S(1)}, f32[512,512]{1,0:T(8,128)}, u32[]{:S(2)}) copy-start(f32[512,512]{1,0:T(8,128)} %constant.11.clone.twist_ref) | copy-start | bytes 3145732
  0.0 47.1 %copy-start.4 = (bf16[256,1024]{1,0:T(8,128)(2,1)S(1)}, bf16[256,1024]{1,0:T(8,128)(2,1)}, u32[]{:S(2)}) copy-start(bf16[256,1024]{1,0:T(8,128)(2,1)} %constant.14.clone.last_ref) | copy-start | bytes 1572868
  0.0 47.1 %copy-start.5 = (bf16[512,512]{1,0:T(8,128)(2,1)S(1)}, bf16[512,512]{1,0:T(8,128)(2,1)}, u32[]{:S(2)}) copy-start(bf16[512,512]{1,0:T(8,128)(2,1)} %constant.10.clone.first_ref) | copy-start | bytes 1572868
  1.8 45.3 %copy-start = (bf16[4,512,256]{2,1,0:T(8,128)(2,1)S(1)}, bf16[4,512,256]{2,1,0:T(8,128)(2,1)}, u32[]{:S(2)}) copy-start(bf16[4,512,256]{2,1,0:T(8,128)(2,1)} %constant.13.clone.back_ref) | copy-start | bytes 3145732
  1.8 45.3 %copy-start.1 = (bf16[4,512,256]{2,1,0:T(8,128)(2,1)S(1)}, bf16[4,512,256]{2,1,0:T(8,128)(2,1)}, u32[]{:S(2)}) copy-start(bf16[4,512,256]{2,1,0:T(8,128)(2,1)} %constant.12.clone.forth_ref) | copy-start | bytes 3145732
  50.9 25.7 %copy-start.3 = (f32[256,512]{1,0:T(8,128)S(1)}, f32[256,512]{1,0:T(8,128)}, u32[]{:S(2)}) copy-start(f32[256,512]{1,0:T(8,128)} %query_ref.1) | copy-start | bytes 1572868

commit v5 on v4

--- a/solution.py
+++ b/solution.py
@@ -80,39 +80,49 @@
     return dot(jnp.concatenate([high, high, low], 1), table)
 
 
-def gate_kernel(key_hbm, value_hbm, filter_hbm, skip_hbm, out_ref, key_ref, value_ref, filter_ref, skip_ref, sems):
+def gate_kernel(key_hbm, value_hbm, filter_hbm, skip_hbm, out_ref, key_ref, value_ref, skip_ref, sems, filter_sems, skip_sem):
     channels, width = key_ref.shape
     blocks = width // LANES
     part = channels // CHUNKS
+    flat = out_ref.reshape(channels * 2 * blocks, LANES)
 
     def copies(i):
         rows = pl.ds(i * part, part)
-        pairs = ((key_hbm, key_ref), (value_hbm, value_ref), (filter_hbm, filter_ref))
+        pairs = ((key_hbm, key_ref), (value_hbm, value_ref))
         return [
             pltpu.make_async_copy(there.at[rows], here.at[rows], sems.at[n, i]) for n, (there, here) in enumerate(pairs)
         ]
 
-    skip_copy = pltpu.make_async_copy(skip_hbm, skip_ref, sems.at[3, 0])
-    skip_copy.start()
     for i in range(CHUNKS):
         for copy in copies(i):
             copy.start()
-    first_device = (lax.axis_index(AXES[0]) == 0) & (lax.axis_index(AXES[1]) == 0)
-    lane = lax.broadcasted_iota(jnp.int32, (part, LANES), 1)
-    first_position = (lane == 0) & first_device
-    skip_copy.wait()
+    filter_copies = [
+        pltpu.make_async_copy(
+            filter_hbm.at[:, pl.ds(q * LANES, LANES)], out_ref.at[:, blocks + q, :], filter_sems.at[q]
+        )
+        for q in range(blocks)
+    ]
+    for copy in filter_copies:
+        copy.start()
+    skip_copy = pltpu.make_async_copy(skip_hbm, skip_ref, skip_sem)
+    skip_copy.start()
     for i in range(CHUNKS):
         for copy in copies(i):
             copy.wait()
         rows = pl.ds(i * part, part)
-        skip = jnp.broadcast_to(skip_ref[:, i * part : (i + 1) * part], (LANES, part)).T
-        skip = jnp.where(first_position, skip, 0.0)
         for q in range(blocks):
             at = pl.ds(q * LANES, LANES)
-            first = i * part * 2 * blocks + q
-            lags = filter_ref[rows, at]
-            out_ref[pl.ds(first, part, stride=2 * blocks), :] = key_ref[rows, at] * value_ref[rows, at]
-            out_ref[pl.ds(first + blocks, part, stride=2 * blocks), :] = lags + skip if q == 0 else lags
+            flat[pl.ds(i * part * 2 * blocks + q, part, stride=2 * blocks), :] = key_ref[rows, at] * value_ref[rows, at]
+    skip_copy.wait()
+    for copy in filter_copies:
+        copy.wait()
+
+    @pl.when((lax.axis_index(AXES[0]) == 0) & (lax.axis_index(AXES[1]) == 0))
+    def _():
+        lane = lax.broadcasted_iota(jnp.int32, (channels, LANES), 1)
+        skip = jnp.broadcast_to(skip_ref[...], (LANES, channels)).T
+        at = pl.ds(blocks, channels, stride=2 * blocks)
+        flat[at, :] = flat[at, :] + jnp.where(lane == 0, skip, 0.0)
 
 
 def four(pairs, sign):
@@ -237,20 +247,19 @@
     ]
     both = pl.pallas_call(
         gate_kernel,
-        out_shape=pltpu.VMEM((channels * 2 * blocks, LANES), jnp.float32),
+        out_shape=pltpu.VMEM((channels, 2 * blocks, LANES), jnp.float32),
         in_specs=[pl.BlockSpec(memory_space=pltpu.HBM)] * 4,
         scratch_shapes=[
             pltpu.VMEM((channels, width), jnp.float32),
             pltpu.VMEM((channels, width), jnp.float32),
-            pltpu.VMEM((channels, width), jnp.float32),
             pltpu.VMEM((1, channels), jnp.float32),
-            pltpu.SemaphoreType.DMA((4, CHUNKS)),
+            pltpu.SemaphoreType.DMA((2, CHUNKS)),
+            pltpu.SemaphoreType.DMA((blocks,)),
+            pltpu.SemaphoreType.DMA,
         ],
         compiler_params=params(16),
     )(*sources)
-    both = lax.all_to_all(
-        both.reshape(channels, 2 * blocks, LANES), AXES, split_axis=0, concat_axis=0, tiled=True
-    )
+    both = lax.all_to_all(both, AXES, split_axis=0, concat_axis=0, tiled=True)
     y = convolve(both.reshape(lines * 2 * blocks, LANES), lines, width)
     y = lax.all_to_all(y.reshape(lines, blocks, LANES), AXES, split_axis=0, concat_axis=0, tiled=True)
     return pl.pallas_call(

time: 78.7 us -> 78.5 us (level)
  no operation moved by 1% of the time
where the time goes in v5:
time: 78.5 us; the launch traced here: 77.3 us
  blocking collectives  71 us (90%)
  Pallas kernels  6.17 us (8%)
    all_to_all x1, blocking collectives, body(): both = lax.all_to_all(both, AXES, split_axis=0, concat_axis=0, tiled=True)  45.3 us
    all_to_all x1, blocking collectives, body(): lax.all_to_all(y.reshape(lines, blocks, LANES), AXES, split_axis=0, conca...  25.7 us
    pallas_call x1, Pallas kernels, convolve(): pl.pallas_call(convolve_kernel, out_shape=jax.ShapeDtypeStruct((lines * R...  3.75 us
    pallas_call x1, Pallas kernels, body(): pl.pallas_call(gate_kernel, out_shape=pltpu.VMEM((channels, 2 * blocks, L...  1.57 us

profile of v5, /device:TPU:16, one launch (start us, length us, event | category | flops | bytes accessed | tf_op | source)
XLA Modules:
  0.0 77.3 jit_solution(2512117106163396956)
XLA Ops:
  0.0 0.0 copy-start.2
  0.0 0.0 copy-start.4
  0.0 0.0 copy-start.5
  0.0 1.6 %shard_map.100 = f32[256,8,128]{2,1,0:T(8,128)S(1)} custom-call(f32[256,512]{1,0:T(8,128)} %key_hbm.1, f32[256,512]{1,0:T(8,128)} %value_hbm.1, f32[256,512]{1,0:T(8,128)} %filter_hbm.1, f32[1,256]{1,0:T(1,128)} %bitcast.7), custom_call_target="tpu_custom_call" | custom-call | tf_op jit(solution)/shard_map/pallas_call | solution.py:248
  1.6 0.0 copy-start
  1.6 0.0 copy-start.1
  1.6 45.3 %all_to_all.10 = f32[256,8,128]{2,1,0:T(8,128)S(1)} all-to-all(f32[256,8,128]{2,1,0:T(8,128)S(1)} %shard_map.100), channel_id=1, replica_groups=mesh['grp'=4,'pos'=64] {'grp','pos'}, dimensions={0} | all-to-all | bytes 2097152 | tf_op jit(solution)/shard_map/all_to_all | solution.py:262
  46.9 0.0 copy-done.2
  46.9 0.0 copy-done.4
  46.9 0.0 copy-done.5
  46.9 0.0 copy-done
  46.9 0.0 copy-done.1
  47.0 3.8 %shard_map.101 = f32[1024,128]{1,0:T(8,128)S(1)} custom-call(f32[2048,128]{1,0:T(8,128)S(1)} %bitcast.4, bf16[512,512]{1,0:T(8,128)(2,1)S(1)} %copy-done.5, f32[512,512]{1,0:T(8,128)S(1)} %copy-done.2, bf16[4,512,256]{2,1,0:T(8,128)(2,1)S(1)} %copy-done.1, bf16[4,512,256]{2,1,0:T(8,128)(2,1)S(1)} %copy-done, bf16[256,1024]{1,0:T(8,128)(2,1)S(1)} %copy-done.4), custom_call_target="tpu_custom_call" | custom-call | tf_op jit(solution)/shard_map/pallas_call | solution.py:225
  50.7 0.0 copy-start.3
  50.7 25.7 %all_to_all.11 = f32[256,4,128]{2,1,0:T(4,128)S(1)} all-to-all(f32[256,4,128]{2,1,0:T(4,128)S(1)} %bitcast.6), channel_id=1, replica_groups=mesh['grp'=4,'pos'=64] {'grp','pos'}, dimensions={0} | all-to-all | bytes 1048576 | tf_op jit(solution)/shard_map/all_to_all | solution.py:264
  76.5 0.0 copy-done.3
  76.5 0.8 %shard_map.102 = f32[256,512]{1,0:T(8,128)} custom-call(f32[256,512]{1,0:T(8,128)S(1)} %copy-done.3, f32[1024,128]{1,0:T(8,128)S(1)} %bitcast.5), custom_call_target="tpu_custom_call" | custom-call | tf_op jit(solution)/shard_map/pallas_call | solution.py:265
Async XLA Ops:
  0.0 46.9 %copy-start.2 = (f32[512,512]{1,0:T(8,128)S(1)}, f32[512,512]{1,0:T(8,128)}, u32[]{:S(2)}) copy-start(f32[512,512]{1,0:T(8,128)} %constant.11.clone.twist_ref) | copy-start | bytes 3145732
  0.0 46.9 %copy-start.4 = (bf16[256,1024]{1,0:T(8,128)(2,1)S(1)}, bf16[256,1024]{1,0:T(8,128)(2,1)}, u32[]{:S(2)}) copy-start(bf16[256,1024]{1,0:T(8,128)(2,1)} %constant.14.clone.last_ref) | copy-start | bytes 1572868
  0.0 46.9 %copy-start.5 = (bf16[512,512]{1,0:T(8,128)(2,1)S(1)}, bf16[512,512]{1,0:T(8,128)(2,1)}, u32[]{:S(2)}) copy-start(bf16[512,512]{1,0:T(8,128)(2,1)} %constant.10.clone.first_ref) | copy-start | bytes 1572868
  1.6 45.3 %copy-start = (bf16[4,512,256]{2,1,0:T(8,128)(2,1)S(1)}, bf16[4,512,256]{2,1,0:T(8,128)(2,1)}, u32[]{:S(2)}) copy-start(bf16[4,512,256]{2,1,0:T(8,128)(2,1)} %constant.13.clone.back_ref) | copy-start | bytes 3145732
  1.6 45.3 %copy-start.1 = (bf16[4,512,256]{2,1,0:T(8,128)(2,1)S(1)}, bf16[4,512,256]{2,1,0:T(8,128)(2,1)}, u32[]{:S(2)}) copy-start(bf16[4,512,256]{2,1,0:T(8,128)(2,1)} %constant.12.clone.forth_ref) | copy-start | bytes 3145732
  50.7 25.7 %copy-start.3 = (f32[256,512]{1,0:T(8,128)S(1)}, f32[256,512]{1,0:T(8,128)}, u32[]{:S(2)}) copy-start(f32[256,512]{1,0:T(8,128)} %query_ref.1) | copy-start | bytes 1572868

commit v6 on v5

--- a/solution.py
+++ b/solution.py
@@ -41,7 +41,12 @@
     length = lines * width
     line = np.arange(lines)
     offset = np.arange(width)
+    half = line[: lines // 2]
     c1, s1 = turns(np.outer(4 * line + 1, line), 4 * lines)
+    last = []
+    for j in range(2):
+        ch, sh = turns(np.outer(2 * half + j, 4 * half + 1), 4 * lines)
+        last.append(table_pair(np.concatenate([ch, -sh], 1), -1))
     ct, st = turns(np.outer(4 * line + 1, offset), 4 * length)
     small = np.arange(width // RADIX)
     forth, back = [], []
@@ -55,7 +60,7 @@
         np.concatenate([ct, st], 0).astype(np.float32),
         table_pair(np.stack(forth), -2),
         table_pair(np.stack(back), -2),
-        table_pair(np.concatenate([c1.T, -s1.T], 1), -1),
+        np.stack(last),
     )
 
 
@@ -138,7 +143,7 @@
 def convolve_kernel(x_ref, first_ref, twist_ref, forth_ref, back_ref, last_ref, y_ref, xh, xl, zh, zl, dh, dl):
     lines = y_ref.shape[0] // RADIX
     width = RADIX * LANES
-    lower, upper = slice(0, lines), slice(lines, 2 * lines)
+    half = lines // 2
 
     def lanes(q):
         return slice(q * LANES, (q + 1) * LANES)
@@ -175,15 +180,23 @@
         gr, gi, fr, fi = g[:, :LANES], g[:, LANES:], f[:, :LANES], f[:, LANES:]
         return split(jnp.concatenate([gr * fr - gi * fi, gr * fi + gi * fr], 1))
 
+    def turned_back(backs, row):
+        pairs = [(back[row : row + STEP, :LANES], back[row : row + STEP, LANES:]) for back in backs]
+        turned = []
+        for q, (re, im) in enumerate(four(pairs, 1)):
+            ct = twist_ref[row : row + STEP, lanes(q)]
+            st = twist_ref[lines + row : lines + row + STEP, lanes(q)]
+            turned.append((re * ct - im * st, im * ct + re * st))
+        return turned
+
     def turn_back(backs):
-        for row in range(0, lines, STEP):
-            rows = slice(row, row + STEP)
-            below = slice(lines + row, lines + row + STEP)
-            pairs = [(back[rows, :LANES], back[rows, LANES:]) for back in backs]
-            for q, (re, im) in enumerate(four(pairs, 1)):
-                ct, st = twist_ref[rows, lanes(q)], twist_ref[below, lanes(q)]
-                dh[rows, lanes(q)], dl[rows, lanes(q)] = split(re * ct - im * st)
-                dh[below, lanes(q)], dl[below, lanes(q)] = split(im * ct + re * st)
+        for row in range(0, half, STEP):
+            both = zip(turned_back(backs, row), turned_back(backs, half + row))
+            for q, (near, far) in enumerate(both):
+                for part in range(2):
+                    at = slice(part * half + row, part * half + row + STEP)
+                    dh[0, at, lanes(q)], dl[0, at, lanes(q)] = split(near[part] + far[part])
+                    dh[1, at, lanes(q)], dl[1, at, lanes(q)] = split(near[part] - far[part])
 
     take(0)
     spread_g = over_lines(0)
@@ -198,11 +211,10 @@
         high, low = product(gs[r], fs[r])
         backs.append(dot_right(high, low, back_ref[r]))
     turn_back(backs)
-    for q in range(0, RADIX, 2):
-        at = slice(q * LANES, (q + 2) * LANES)
-        y = dot_left(last_ref[...], dh[:, at], dl[:, at])
-        y_ref[pl.ds(q, lines, stride=RADIX), :] = y[:, :LANES]
-        y_ref[pl.ds(q + 1, lines, stride=RADIX), :] = y[:, LANES:]
+    for j in range(2):
+        y = dot_left(last_ref[j], dh[j], dl[j])
+        for q in range(RADIX):
+            y_ref[pl.ds(j * RADIX + q, half, stride=2 * RADIX), :] = y[:, lanes(q)]
 
 
 def mix_kernel(query_ref, y_ref, out_hbm, out_ref, sems):
@@ -230,8 +242,8 @@
             pltpu.VMEM((lines, 2 * width), jnp.bfloat16),
             pltpu.VMEM((RADIX, 2 * lines, 2 * LANES), jnp.bfloat16),
             pltpu.VMEM((RADIX, 2 * lines, 2 * LANES), jnp.bfloat16),
-            pltpu.VMEM((2 * lines, width), jnp.bfloat16),
-            pltpu.VMEM((2 * lines, width), jnp.bfloat16),
+            pltpu.VMEM((2, lines, width), jnp.bfloat16),
+            pltpu.VMEM((2, lines, width), jnp.bfloat16),
         ],
         compiler_params=params(32),
     )(x, *tables(lines, width))

time: 78.5 us -> 78.3 us (level)
  no operation moved by 1% of the time
where the time goes in v6:
time: 78.3 us; the launch traced here: 77.1 us
  blocking collectives  71 us (91%)
  Pallas kernels  5.95 us (8%)
    all_to_all x1, blocking collectives, body(): both = lax.all_to_all(both, AXES, split_axis=0, concat_axis=0, tiled=True)  45.3 us
    all_to_all x1, blocking collectives, body(): lax.all_to_all(y.reshape(lines, blocks, LANES), AXES, split_axis=0, conca...  25.7 us
    pallas_call x1, Pallas kernels, convolve(): pl.pallas_call(convolve_kernel, out_shape=jax.ShapeDtypeStruct((lines * R...  3.55 us

profile of v6, /device:TPU:16, one launch (start us, length us, event | category | flops | bytes accessed | tf_op | source)
XLA Modules:
  0.0 77.1 jit_solution(1347409476585351981)
XLA Ops:
  0.0 0.0 copy-start.2
  0.0 0.0 copy-start.4
  0.0 0.0 copy-start.5
  0.0 1.6 %shard_map.100 = f32[256,8,128]{2,1,0:T(8,128)S(1)} custom-call(f32[256,512]{1,0:T(8,128)} %key_hbm.1, f32[256,512]{1,0:T(8,128)} %value_hbm.1, f32[256,512]{1,0:T(8,128)} %filter_hbm.1, f32[1,256]{1,0:T(1,128)} %bitcast.7), custom_call_target="tpu_custom_call" | custom-call | tf_op jit(solution)/shard_map/pallas_call | solution.py:260
  1.6 0.0 copy-start
  1.6 0.0 copy-start.1
  1.6 45.3 %all_to_all.10 = f32[256,8,128]{2,1,0:T(8,128)S(1)} all-to-all(f32[256,8,128]{2,1,0:T(8,128)S(1)} %shard_map.100), channel_id=1, replica_groups=mesh['grp'=4,'pos'=64] {'grp','pos'}, dimensions={0} | all-to-all | bytes 2097152 | tf_op jit(solution)/shard_map/all_to_all | solution.py:274
  46.9 0.0 copy-done.2
  46.9 0.0 copy-done.4
  46.9 0.0 copy-done.5
  46.9 0.0 copy-done
  46.9 0.0 copy-done.1
  46.9 3.6 %shard_map.101 = f32[1024,128]{1,0:T(8,128)S(1)} custom-call(f32[2048,128]{1,0:T(8,128)S(1)} %bitcast.4, bf16[512,512]{1,0:T(8,128)(2,1)S(1)} %copy-done.4, f32[512,512]{1,0:T(8,128)S(1)} %copy-done.2, bf16[4,512,256]{2,1,0:T(8,128)(2,1)S(1)} %copy-done.1, bf16[4,512,256]{2,1,0:T(8,128)(2,1)S(1)} %copy-done, bf16[2,128,512]{2,1,0:T(8,128)(2,1)S(1)} %copy-done.5), custom_call_target="tpu_custom_call" | custom-call | tf_op jit(solution)/shard_map/pallas_call | solution.py:237
  50.5 0.0 copy-start.3
  50.5 25.7 %all_to_all.11 = f32[256,4,128]{2,1,0:T(4,128)S(1)} all-to-all(f32[256,4,128]{2,1,0:T(4,128)S(1)} %bitcast.6), channel_id=1, replica_groups=mesh['grp'=4,'pos'=64] {'grp','pos'}, dimensions={0} | all-to-all | bytes 1048576 | tf_op jit(solution)/shard_map/all_to_all | solution.py:276
  76.2 0.0 copy-done.3
  76.2 0.8 %shard_map.102 = f32[256,512]{1,0:T(8,128)} custom-call(f32[256,512]{1,0:T(8,128)S(1)} %copy-done.3, f32[1024,128]{1,0:T(8,128)S(1)} %bitcast.5), custom_call_target="tpu_custom_call" | custom-call | tf_op jit(solution)/shard_map/pallas_call | solution.py:277
Async XLA Ops:
  0.0 46.9 %copy-start.2 = (f32[512,512]{1,0:T(8,128)S(1)}, f32[512,512]{1,0:T(8,128)}, u32[]{:S(2)}) copy-start(f32[512,512]{1,0:T(8,128)} %constant.11.clone.twist_ref) | copy-start | bytes 3145732
  0.0 46.9 %copy-start.4 = (bf16[512,512]{1,0:T(8,128)(2,1)S(1)}, bf16[512,512]{1,0:T(8,128)(2,1)}, u32[]{:S(2)}) copy-start(bf16[512,512]{1,0:T(8,128)(2,1)} %constant.10.clone.first_ref) | copy-start | bytes 1572868
  0.0 46.9 %copy-start.5 = (bf16[2,128,512]{2,1,0:T(8,128)(2,1)S(1)}, bf16[2,128,512]{2,1,0:T(8,128)(2,1)}, u32[]{:S(2)}) copy-start(bf16[2,128,512]{2,1,0:T(8,128)(2,1)} %constant.14.clone.last_ref) | copy-start | bytes 786436
  1.6 45.3 %copy-start = (bf16[4,512,256]{2,1,0:T(8,128)(2,1)S(1)}, bf16[4,512,256]{2,1,0:T(8,128)(2,1)}, u32[]{:S(2)}) copy-start(bf16[4,512,256]{2,1,0:T(8,128)(2,1)} %constant.13.clone.back_ref) | copy-start | bytes 3145732
  1.6 45.3 %copy-start.1 = (bf16[4,512,256]{2,1,0:T(8,128)(2,1)S(1)}, bf16[4,512,256]{2,1,0:T(8,128)(2,1)}, u32[]{:S(2)}) copy-start(bf16[4,512,256]{2,1,0:T(8,128)(2,1)} %constant.12.clone.forth_ref) | copy-start | bytes 3145732
  50.5 25.7 %copy-start.3 = (f32[256,512]{1,0:T(8,128)S(1)}, f32[256,512]{1,0:T(8,128)}, u32[]{:S(2)}) copy-start(f32[256,512]{1,0:T(8,128)} %query_ref.1) | copy-start | bytes 1572868

commit v7 on v6

--- a/solution.py
+++ b/solution.py
@@ -42,9 +42,10 @@
     line = np.arange(lines)
     offset = np.arange(width)
     half = line[: lines // 2]
-    c1, s1 = turns(np.outer(4 * line + 1, line), 4 * lines)
-    last = []
+    first, last = [], []
     for j in range(2):
+        ch, sh = turns(np.outer(4 * half + 1, 2 * half + j), 4 * lines)
+        first.append(table_pair(np.concatenate([ch, -sh], 0), -1))
         ch, sh = turns(np.outer(2 * half + j, 4 * half + 1), 4 * lines)
         last.append(table_pair(np.concatenate([ch, -sh], 1), -1))
     ct, st = turns(np.outer(4 * line + 1, offset), 4 * length)
@@ -56,7 +57,7 @@
         forth.append(block)
         back.append(block.T / length)
     return (
-        table_pair(np.concatenate([c1, -s1], 0), -1),
+        np.stack(first),
         np.concatenate([ct, st], 0).astype(np.float32),
         table_pair(np.stack(forth), -2),
         table_pair(np.stack(back), -2),
@@ -150,23 +151,32 @@
 
     def take(signal):
         for q in range(RADIX):
-            j = signal * RADIX + q
-            xh[:, lanes(j)], xl[:, lanes(j)] = split(x_ref[pl.ds(j, lines, stride=2 * RADIX), :])
+            n = signal * RADIX + q
+            for j in range(2):
+                at = slice(j * half, (j + 1) * half)
+                xh[at, lanes(n)], xl[at, lanes(n)] = split(
+                    x_ref[pl.ds(2 * RADIX * j + n, half, stride=4 * RADIX), :]
+                )
 
     def over_lines(signal):
         at = slice(signal * width, (signal + 1) * width)
-        return dot_left(first_ref[...], xh[:, at], xl[:, at])
+        spread = []
+        for j in range(2):
+            rows = slice(j * half, (j + 1) * half)
+            spread.append(dot_left(first_ref[j], xh[rows, at], xl[rows, at]))
+        return spread
 
     def turn(signal, spread):
-        at = slice(signal * lines, (signal + 1) * lines)
+        even, odd = spread
         for row in range(0, lines, STEP):
-            rows = slice(row, row + STEP)
-            below = slice(lines + row, lines + row + STEP)
             here = slice(signal * lines + row, signal * lines + row + STEP)
+            k = row % half
             pairs = []
             for q in range(RADIX):
-                re, im = spread[rows, lanes(q)], spread[below, lanes(q)]
-                ct, st = twist_ref[rows, lanes(q)], twist_ref[below, lanes(q)]
+                er, ei = even[k : k + STEP, lanes(q)], even[half + k : half + k + STEP, lanes(q)]
+                fr, fi = odd[k : k + STEP, lanes(q)], odd[half + k : half + k + STEP, lanes(q)]
+                re, im = (er + fr, ei + fi) if row < half else (er - fr, ei - fi)
+                ct, st = twist_ref[row : row + STEP, lanes(q)], twist_ref[lines + row : lines + row + STEP, lanes(q)]
                 pairs.append((re * ct + im * st, im * ct - re * st))
             for r, pair in enumerate(four(pairs, -1)):
                 for part, value in enumerate(pair):
@@ -190,13 +200,15 @@
         return turned
 
     def turn_back(backs):
+        later = []
         for row in range(0, half, STEP):
             both = zip(turned_back(backs, row), turned_back(backs, half + row))
             for q, (near, far) in enumerate(both):
                 for part in range(2):
                     at = slice(part * half + row, part * half + row + STEP)
                     dh[0, at, lanes(q)], dl[0, at, lanes(q)] = split(near[part] + far[part])
-                    dh[1, at, lanes(q)], dl[1, at, lanes(q)] = split(near[part] - far[part])
+                    later.append((at, lanes(q), near[part] - far[part]))
+        return later
 
     take(0)
     spread_g = over_lines(0)
@@ -208,11 +220,18 @@
     fs = [over_offsets(1, r) for r in range(RADIX)]
     backs = []
     for r in range(RADIX):
-        high, low = product(gs[r], fs[r])
-        backs.append(dot_right(high, low, back_ref[r]))
-    turn_back(backs)
+        parts = []
+        for k in range(0, lines, half):
+            rows = slice(k, k + half)
+            high, low = product(gs[r][rows], fs[r][rows])
+            parts.append(dot_right(high, low, back_ref[r]))
+        backs.append(jnp.concatenate(parts, 0))
+    later = turn_back(backs)
     for j in range(2):
         y = dot_left(last_ref[j], dh[j], dl[j])
+        if j == 0:
+            for rows, at, value in later:
+                dh[1, rows, at], dl[1, rows, at] = split(value)
         for q in range(RADIX):
             y_ref[pl.ds(j * RADIX + q, half, stride=2 * RADIX), :] = y[:, lanes(q)]
 

time: 78.3 us -> 78.2 us (level)
  no operation moved by 1% of the time
where the time goes in v7:
time: 78.2 us; the launch traced here: 77 us
  blocking collectives  71 us (91%)
  Pallas kernels  5.89 us (8%)
    all_to_all x1, blocking collectives, body(): both = lax.all_to_all(both, AXES, split_axis=0, concat_axis=0, tiled=True)  45.3 us
    all_to_all x1, blocking collectives, body(): lax.all_to_all(y.reshape(lines, blocks, LANES), AXES, split_axis=0, conca...  25.7 us
    pallas_call x1, Pallas kernels, convolve(): pl.pallas_call(convolve_kernel, out_shape=jax.ShapeDtypeStruct((lines * R...  3.51 us

profile of v7, /device:TPU:16, one launch (start us, length us, event | category | flops | bytes accessed | tf_op | source)
XLA Modules:
  0.0 77.0 jit_solution(1821319750233139407)
XLA Ops:
  0.0 0.0 copy-start.2
  0.0 0.0 copy-start.4
  0.0 0.0 copy-start.5
  0.0 1.5 %shard_map.100 = f32[256,8,128]{2,1,0:T(8,128)S(1)} custom-call(f32[256,512]{1,0:T(8,128)} %key_hbm.1, f32[256,512]{1,0:T(8,128)} %value_hbm.1, f32[256,512]{1,0:T(8,128)} %filter_hbm.1, f32[1,256]{1,0:T(1,128)} %bitcast.7), custom_call_target="tpu_custom_call" | custom-call | tf_op jit(solution)/shard_map/pallas_call | solution.py:279
  1.6 0.0 copy-start
  1.6 0.0 copy-start.1
  1.6 45.3 %all_to_all.10 = f32[256,8,128]{2,1,0:T(8,128)S(1)} all-to-all(f32[256,8,128]{2,1,0:T(8,128)S(1)} %shard_map.100), channel_id=1, replica_groups=mesh['grp'=4,'pos'=64] {'grp','pos'}, dimensions={0} | all-to-all | bytes 2097152 | tf_op jit(solution)/shard_map/all_to_all | solution.py:293
  46.9 0.0 copy-done.2
  46.9 0.0 copy-done.4
  46.9 0.0 copy-done.5
  46.9 0.0 copy-done
  46.9 0.0 copy-done.1
  46.9 3.5 %shard_map.101 = f32[1024,128]{1,0:T(8,128)S(1)} custom-call(f32[2048,128]{1,0:T(8,128)S(1)} %bitcast.4, bf16[2,256,256]{2,1,0:T(8,128)(2,1)S(1)} %copy-done.5, f32[512,512]{1,0:T(8,128)S(1)} %copy-done.2, bf16[4,512,256]{2,1,0:T(8,128)(2,1)S(1)} %copy-done.1, bf16[4,512,256]{2,1,0:T(8,128)(2,1)S(1)} %copy-done, bf16[2,128,512]{2,1,0:T(8,128)(2,1)S(1)} %copy-done.4), custom_call_target="tpu_custom_call" | custom-call | tf_op jit(solution)/shard_map/pallas_call | solution.py:256
  50.4 0.0 copy-start.3
  50.5 25.7 %all_to_all.11 = f32[256,4,128]{2,1,0:T(4,128)S(1)} all-to-all(f32[256,4,128]{2,1,0:T(4,128)S(1)} %bitcast.5), channel_id=1, replica_groups=mesh['grp'=4,'pos'=64] {'grp','pos'}, dimensions={0} | all-to-all | bytes 1048576 | tf_op jit(solution)/shard_map/all_to_all | solution.py:295
  76.2 0.0 copy-done.3
  76.2 0.8 %shard_map.102 = f32[256,512]{1,0:T(8,128)} custom-call(f32[256,512]{1,0:T(8,128)S(1)} %copy-done.3, f32[1024,128]{1,0:T(8,128)S(1)} %bitcast.6), custom_call_target="tpu_custom_call" | custom-call | tf_op jit(solution)/shard_map/pallas_call | solution.py:296
Async XLA Ops:
  0.0 46.9 %copy-start.2 = (f32[512,512]{1,0:T(8,128)S(1)}, f32[512,512]{1,0:T(8,128)}, u32[]{:S(2)}) copy-start(f32[512,512]{1,0:T(8,128)} %constant.11.clone.twist_ref) | copy-start | bytes 3145732
  0.0 46.9 %copy-start.4 = (bf16[2,128,512]{2,1,0:T(8,128)(2,1)S(1)}, bf16[2,128,512]{2,1,0:T(8,128)(2,1)}, u32[]{:S(2)}) copy-start(bf16[2,128,512]{2,1,0:T(8,128)(2,1)} %constant.14.clone.last_ref) | copy-start | bytes 786436
  0.0 46.9 %copy-start.5 = (bf16[2,256,256]{2,1,0:T(8,128)(2,1)S(1)}, bf16[2,256,256]{2,1,0:T(8,128)(2,1)}, u32[]{:S(2)}) copy-start(bf16[2,256,256]{2,1,0:T(8,128)(2,1)} %constant.10.clone.first_ref) | copy-start | bytes 786436
  1.6 45.3 %copy-start = (bf16[4,512,256]{2,1,0:T(8,128)(2,1)S(1)}, bf16[4,512,256]{2,1,0:T(8,128)(2,1)}, u32[]{:S(2)}) copy-start(bf16[4,512,256]{2,1,0:T(8,128)(2,1)} %constant.13.clone.back_ref) | copy-start | bytes 3145732
  1.6 45.3 %copy-start.1 = (bf16[4,512,256]{2,1,0:T(8,128)(2,1)S(1)}, bf16[4,512,256]{2,1,0:T(8,128)(2,1)}, u32[]{:S(2)}) copy-start(bf16[4,512,256]{2,1,0:T(8,128)(2,1)} %constant.12.clone.forth_ref) | copy-start | bytes 3145732
  50.4 25.7 %copy-start.3 = (f32[256,512]{1,0:T(8,128)S(1)}, f32[256,512]{1,0:T(8,128)}, u32[]{:S(2)}) copy-start(f32[256,512]{1,0:T(8,128)} %query_ref.1) | copy-start | bytes 1572868

commit v8 on v7

--- a/solution.py
+++ b/solution.py
@@ -166,9 +166,9 @@
             spread.append(dot_left(first_ref[j], xh[rows, at], xl[rows, at]))
         return spread
 
-    def turn(signal, spread):
+    def turn(signal, spread, start=0, stop=lines):
         even, odd = spread
-        for row in range(0, lines, STEP):
+        for row in range(start, stop, STEP):
             here = slice(signal * lines + row, signal * lines + row + STEP)
             k = row % half
             pairs = []
@@ -215,8 +215,10 @@
     take(1)
     spread_f = over_lines(1)
     turn(0, spread_g)
-    gs = [over_offsets(0, r) for r in range(RADIX)]
-    turn(1, spread_f)
+    gs = []
+    for r in range(RADIX):
+        turn(1, spread_f, r * lines // RADIX, (r + 1) * lines // RADIX)
+        gs.append(over_offsets(0, r))
     fs = [over_offsets(1, r) for r in range(RADIX)]
     backs = []
     for r in range(RADIX):

time: 78.2 us -> 78.2 us (level)
  no operation moved by 1% of the time
where the time goes in v8:
time: 78.2 us; the launch traced here: 77 us
  blocking collectives  71 us (91%)
  Pallas kernels  5.89 us (8%)
    all_to_all x1, blocking collectives, body(): both = lax.all_to_all(both, AXES, split_axis=0, concat_axis=0, tiled=True)  45.3 us
    all_to_all x1, blocking collectives, body(): lax.all_to_all(y.reshape(lines, blocks, LANES), AXES, split_axis=0, conca...  25.7 us
    pallas_call x1, Pallas kernels, convolve(): pl.pallas_call(convolve_kernel, out_shape=jax.ShapeDtypeStruct((lines * R...  3.51 us

profile of v8, /device:TPU:16, one launch (start us, length us, event | category | flops | bytes accessed | tf_op | source)
XLA Modules:
  0.0 77.0 jit_solution(15185250828332443125)
XLA Ops:
  0.0 0.0 copy-start.2
  0.0 0.0 copy-start.4
  0.0 0.0 copy-start.5
  0.0 1.5 %shard_map.100 = f32[256,8,128]{2,1,0:T(8,128)S(1)} custom-call(f32[256,512]{1,0:T(8,128)} %key_hbm.1, f32[256,512]{1,0:T(8,128)} %value_hbm.1, f32[256,512]{1,0:T(8,128)} %filter_hbm.1, f32[1,256]{1,0:T(1,128)} %bitcast.7), custom_call_target="tpu_custom_call" | custom-call | tf_op jit(solution)/shard_map/pallas_call | solution.py:281
  1.6 0.0 copy-start
  1.6 0.0 copy-start.1
  1.6 45.3 %all_to_all.10 = f32[256,8,128]{2,1,0:T(8,128)S(1)} all-to-all(f32[256,8,128]{2,1,0:T(8,128)S(1)} %shard_map.100), channel_id=1, replica_groups=mesh['grp'=4,'pos'=64] {'grp','pos'}, dimensions={0} | all-to-all | bytes 2097152 | tf_op jit(solution)/shard_map/all_to_all | solution.py:295
  46.9 0.0 copy-done.2
  46.9 0.0 copy-done.4
  46.9 0.0 copy-done.5
  46.9 0.0 copy-done
  46.9 0.0 copy-done.1
  46.9 3.5 %shard_map.101 = f32[1024,128]{1,0:T(8,128)S(1)} custom-call(f32[2048,128]{1,0:T(8,128)S(1)} %bitcast.4, bf16[2,256,256]{2,1,0:T(8,128)(2,1)S(1)} %copy-done.5, f32[512,512]{1,0:T(8,128)S(1)} %copy-done.2, bf16[4,512,256]{2,1,0:T(8,128)(2,1)S(1)} %copy-done.1, bf16[4,512,256]{2,1,0:T(8,128)(2,1)S(1)} %copy-done, bf16[2,128,512]{2,1,0:T(8,128)(2,1)S(1)} %copy-done.4), custom_call_target="tpu_custom_call" | custom-call | tf_op jit(solution)/shard_map/pallas_call | solution.py:258
  50.4 0.0 copy-start.3
  50.5 25.7 %all_to_all.11 = f32[256,4,128]{2,1,0:T(4,128)S(1)} all-to-all(f32[256,4,128]{2,1,0:T(4,128)S(1)} %bitcast.5), channel_id=1, replica_groups=mesh['grp'=4,'pos'=64] {'grp','pos'}, dimensions={0} | all-to-all | bytes 1048576 | tf_op jit(solution)/shard_map/all_to_all | solution.py:297
  76.2 0.0 copy-done.3
  76.2 0.8 %shard_map.102 = f32[256,512]{1,0:T(8,128)} custom-call(f32[256,512]{1,0:T(8,128)S(1)} %copy-done.3, f32[1024,128]{1,0:T(8,128)S(1)} %bitcast.6), custom_call_target="tpu_custom_call" | custom-call | tf_op jit(solution)/shard_map/pallas_call | solution.py:298
Async XLA Ops:
  0.0 46.9 %copy-start.2 = (f32[512,512]{1,0:T(8,128)S(1)}, f32[512,512]{1,0:T(8,128)}, u32[]{:S(2)}) copy-start(f32[512,512]{1,0:T(8,128)} %constant.11.clone.twist_ref) | copy-start | bytes 3145732
  0.0 46.9 %copy-start.4 = (bf16[2,128,512]{2,1,0:T(8,128)(2,1)S(1)}, bf16[2,128,512]{2,1,0:T(8,128)(2,1)}, u32[]{:S(2)}) copy-start(bf16[2,128,512]{2,1,0:T(8,128)(2,1)} %constant.14.clone.last_ref) | copy-start | bytes 786436
  0.0 46.9 %copy-start.5 = (bf16[2,256,256]{2,1,0:T(8,128)(2,1)S(1)}, bf16[2,256,256]{2,1,0:T(8,128)(2,1)}, u32[]{:S(2)}) copy-start(bf16[2,256,256]{2,1,0:T(8,128)(2,1)} %constant.10.clone.first_ref) | copy-start | bytes 786436
  1.6 45.3 %copy-start = (bf16[4,512,256]{2,1,0:T(8,128)(2,1)S(1)}, bf16[4,512,256]{2,1,0:T(8,128)(2,1)}, u32[]{:S(2)}) copy-start(bf16[4,512,256]{2,1,0:T(8,128)(2,1)} %constant.13.clone.back_ref) | copy-start | bytes 3145732
  1.6 45.3 %copy-start.1 = (bf16[4,512,256]{2,1,0:T(8,128)(2,1)S(1)}, bf16[4,512,256]{2,1,0:T(8,128)(2,1)}, u32[]{:S(2)}) copy-start(bf16[4,512,256]{2,1,0:T(8,128)(2,1)} %constant.12.clone.forth_ref) | copy-start | bytes 3145732
  50.4 25.7 %copy-start.3 = (f32[256,512]{1,0:T(8,128)S(1)}, f32[256,512]{1,0:T(8,128)}, u32[]{:S(2)}) copy-start(f32[256,512]{1,0:T(8,128)} %query_ref.1) | copy-start | bytes 1572868
